TPU v7x, 32 devices: a whole 2x2x4 slice. The times are simulated.
32 devices in a mesh: grp: 4 (over x, core), dev: 8 (over z, y).
Axes of the slice: x: 2, y: 2, z: 4, core: 2. Of those that a mesh axis runs over, the one named last changes fastest.
Arguments:
- tensor_slab: bfloat16 [512, 512, 32, 64], P(None, 'dev', 'grp'), may hold values from -400 to 400
- mode_factor: bfloat16 [512, 64], replicated, may hold values from -40 to 40
Outputs:
- triangle: float32 [512, 512], P('dev', 'grp')
All inputs are finite; a program needn't handle non-finite values.
Results may differ from a plain program's by a relative error of at most 0.00033.
Values may be sent and summed in bfloat16 or wider, within the bound.
No kernel may reach another device: no remote copies, remote signals or barrier semaphores. Data moves between devices by JAX's collectives and lax.ppermute only.
A program may use at most 64 MiB of HBM per device.

v0:
```python
import jax
import jax.numpy as jnp
from jax import lax
from jax.sharding import PartitionSpec as P


def own_block(full_tri):
    order = full_tri.shape[0]
    row_count = order // lax.axis_size("dev")
    col_count = order // lax.axis_size("grp")
    row_start = lax.axis_index("dev") * row_count
    col_start = lax.axis_index("grp") * col_count
    return lax.dynamic_slice(full_tri, (row_start, col_start), (row_count, col_count))


def per_device(tensor_slab, mode_factor):
    row_width = tensor_slab.shape[0]
    local_cols = tensor_slab.shape[1]
    slab_depth = tensor_slab.shape[2]
    species = tensor_slab.shape[3]
    flat_slab = tensor_slab.reshape(row_width, local_cols * slab_depth * species)
    projected = lax.dot_general(
        mode_factor, flat_slab, (((0,), (0,)), ((), ())), preferred_element_type=jnp.float32
    )
    projected = projected.astype(jnp.bfloat16).reshape(
        mode_factor.shape[1], local_cols, slab_depth * species
    )
    regrouped = lax.all_to_all(projected, "dev", split_axis=0, concat_axis=1, tiled=True)
    gram_local = lax.dot_general(
        regrouped, regrouped, (((0, 2), (0, 2)), ((), ())), preferred_element_type=jnp.float32
    )
    row_total = mode_factor.shape[1] * slab_depth * species * lax.axis_size("grp")
    gram_local = gram_local / row_total
    gram_total = lax.psum(gram_local, ("grp", "dev"))
    return own_block(jnp.linalg.cholesky(gram_total).T)


def solution(mesh):
    in_specs = (P(None, "dev", "grp", None), P())
    out_specs = P("dev", "grp")
    return jax.shard_map(
        per_device, mesh=mesh, in_specs=in_specs, out_specs=out_specs, check_vma=False
    )
```

profile of v0, /device:TPU:0, one launch (start us, length us, event | category | flops | bytes accessed | tf_op | source)
XLA Modules:
  0.0 352.0 jit_solution(18196734176560616764)
XLA Ops:
  6.5 0.0 copy-start
  6.5 0.0 all-reduce.3.cloned.1.call-start
  6.5 0.8 copy-done
  7.4 15.4 %convolution_convert_fusion = bf16[64,32768]{1,0:T(8,128)(2,1)S(1)} fusion(bf16[512,64]{0,1:T(8,128)(2,1)S(1)} %copy-done, bf16[512,32768]{0,1:T(8,128)(2,1)} %bitcast.37), kind=kOutput, calls=%fused_computation | convolution fusion | flops 2149580800 | bytes 37814272 | tf_op jit(solution)/shard_map/dot_general | solution.py:22
  22.7 1.7 copy.14
  24.4 100.3 %all_to_all.18 = bf16[64,64,512]{2,1,0:T(8,128)(2,1)S(1)} all-to-all(bf16[64,64,512]{2,1,0:T(8,128)(2,1)S(1)} %bitcast.39), channel_id=1, replica_groups=mesh['grp'=4,'dev'=8] {'dev'}, dimensions={0} | all-to-all | bytes 8388608 | tf_op jit(solution)/shard_map/all_to_all | solution.py:28
  124.7 0.5 copy.3
  125.2 3.4 fusion
  128.6 0.0 all-reduce.3.cloned.1.call-update
  128.6 129.0 %all-reduce.3.cloned.1.call-done = f32[512,512]{0,1:T(8,128)} async-done(((f32[512,512]{0,1:T(8,128)}), f32[512,512]{0,1:T(8,128)}) %all-reduce.3.cloned.1.call-update) | async-done | bytes 1048592 | tf_op jit(solution)/shard_map/psum | solution.py:34
  257.6 1.6 copy.5
  259.2 1.4 fusion.1
  260.7 11.7 %cholesky.104 = f32[128,128]{1,0:T(8,128)S(1)} custom-call(f32[128,128]{1,0:T(8,128)S(1)} %cholesky.266), custom_call_target="Cholesky" | custom-call | tf_op jit(solution)/shard_map/jit(cholesky)/cholesky | solution.py:35
  272.4 9.8 %custom-call.27 = f32[1,128,128]{1,2,0:T(8,128)S(1)} custom-call(f32[1,128,128]{2,1,0:T(8,128)S(1)} %get-tuple-element.14), custom_call_target="InvertDiagBlocksLowerTriangular" | custom-call | tf_op jit(solution)/shard_map/jit(cholesky)/cholesky | solution.py:35
  282.2 0.4 fusion.4
  282.6 0.1 copy.6
  282.8 0.5 convolution_subtract_fusion
  283.3 0.1 cholesky.224
  283.4 11.9 %cholesky.217 = f32[128,128]{1,0:T(8,128)S(1)} custom-call(f32[128,128]{1,0:T(8,128)S(1)} %cholesky.270), custom_call_target="Cholesky" | custom-call | tf_op jit(solution)/shard_map/jit(cholesky)/cholesky | solution.py:35
  295.4 9.8 %custom-call.28 = f32[1,128,128]{1,2,0:T(8,128)S(1)} custom-call(f32[1,128,128]{2,1,0:T(8,128)S(1)} %get-tuple-element.11), custom_call_target="InvertDiagBlocksLowerTriangular" | custom-call | tf_op jit(solution)/shard_map/jit(cholesky)/cholesky | solution.py:35
  305.2 0.3 convolution_dynamic-update-slice_fusion
  305.5 0.4 convolution_subtract_fusion.1
  305.9 11.7 %cholesky.238 = f32[128,128]{1,0:T(8,128)S(1)} custom-call(f32[128,128]{1,0:T(8,128)S(1)} %cholesky.275), custom_call_target="Cholesky" | custom-call | tf_op jit(solution)/shard_map/jit(cholesky)/cholesky | solution.py:35
  317.6 0.7 compare_reduce_fusion.1
  318.3 9.8 %custom-call.29 = f32[1,128,128]{1,2,0:T(8,128)S(1)} custom-call(f32[1,128,128]{2,1,0:T(8,128)S(1)} %get-tuple-element.8), custom_call_target="InvertDiagBlocksLowerTriangular" | custom-call | tf_op jit(solution)/shard_map/jit(cholesky)/cholesky | solution.py:35
  328.2 0.2 convolution_dynamic-update-slice_fusion.1
  328.4 0.4 convolution_subtract_fusion.2
  328.8 11.7 %cholesky.255 = f32[128,128]{1,0:T(8,128)S(1)} custom-call(f32[128,128]{1,0:T(8,128)S(1)} %convolution_subtract_fusion.2), custom_call_target="Cholesky" | custom-call | tf_op jit(solution)/shard_map/jit(cholesky)/cholesky | solution.py:35
  340.5 0.6 compare_reduce_fusion
  341.1 0.7 compare_reduce_fusion.2
  344.3 0.1 fusion.9
  344.4 0.7 copy.9
  (8 shorter events, 0.2 us)
Async XLA Ops:
  6.5 0.8 copy-start
  6.5 251.1 %all-reduce.3.cloned.1.call-start = ((), (), s32[]{:S(2)}) async-start(), calls=%async_computation.1 | async-start | bytes 2097152 | tf_op jit(solution)/shard_map/psum | solution.py:34
Sparse Core Ops, SparseCore 0:
  128.7 128.8 all-reduce.2
where the time goes:
time: 352 us
  waiting for transfers between devices  129 us (37%)
  blocking collectives  100 us (28%)
  other arithmetic  80.2 us (23%)
  matrix products  20.9 us (6%)
  between operations  16.1 us (5%)
  local copies, waits for them, and re-layouts  5.52 us (2%)
    psum x1, waiting for transfers between devices, per_device(): gram_total = lax.psum(gram_local, ('grp', 'dev'))  129 us
    all_to_all x1, blocking collectives, per_device(): lax.all_to_all(projected, 'dev', split_axis=0, concat_axis=1, tiled=True)  100 us
    another operation x14, other arithmetic, per_device(): return own_block(jnp.linalg.cholesky(gram_total).T)  78.7 us
    dot_general x1, matrix products, per_device(): lax.dot_general(mode_factor, flat_slab, (((0,), (0,)), ((), ())), preferr...  15.4 us
  transfers between devices with their start and end apart: 1, of which 1 were waited for; matrix products, arithmetic and copies ran while one was open for 0% of the time, Pallas kernels for 0%

commit v1 on v0

v1 whole, which is shorter than its diff:
```python
import functools

import jax
import jax.numpy as jnp
from jax import lax
from jax.experimental import pallas as pl
from jax.experimental.pallas import tpu as pltpu
from jax.sharding import PartitionSpec as P

LANES = 128


def project_kernel(rank, dest_ref, slab_ref, factor_ref, out_ref, wide_ref):
    cols, width, depth = slab_ref.shape
    half = width // 2
    flat = slab_ref[...].reshape(cols * width, depth)
    wide_ref[...] = jnp.dot(flat, factor_ref[...], preferred_element_type=jnp.float32)
    lane = lax.broadcasted_iota(jnp.int32, (cols, LANES), 1)
    for s in range(half):
        low = wide_ref[pl.ds(s, cols, stride=width), :]
        high = wide_ref[pl.ds(s + half, cols, stride=width), :]
        both = jnp.where(lane < rank, low, high)
        out_ref[:, s * LANES:(s + 1) * LANES] = both.astype(out_ref.dtype)


def project(slab, factor_pair, rank, dest, width):
    cols, total_width, depth = slab.shape
    block_cols = 16
    out_width = width * rank
    grid_spec = pltpu.PrefetchScalarGridSpec(
        num_scalar_prefetch=1,
        grid=(cols // block_cols,),
        in_specs=[
            pl.BlockSpec((block_cols, width, depth), lambda c, d: (c, d[0], 0)),
            pl.BlockSpec(factor_pair.shape, lambda c, d: (0, 0)),
        ],
        out_specs=pl.BlockSpec((block_cols, out_width), lambda c, d: (c, 0)),
        scratch_shapes=[pltpu.VMEM((block_cols * width, LANES), jnp.float32)],
    )
    return pl.pallas_call(
        functools.partial(project_kernel, rank),
        out_shape=jax.ShapeDtypeStruct((cols, out_width), jnp.bfloat16),
        grid_spec=grid_spec,
        compiler_params=pltpu.CompilerParams(vmem_limit_bytes=44 * 2**20),
        cost_estimate=pl.CostEstimate(
            flops=8 * cols * width * depth * rank,
            bytes_accessed=2 * cols * width * depth + 2 * cols * out_width,
            transcendentals=0,
        ),
        name="project",
    )(dest.reshape(1), slab, factor_pair)


def lower_blocks(count):
    return [(a, b) for a in range(count) for b in range(a + 1)]


def gram_kernel(scale, count, place_ref, *refs):
    pieces = refs[:count]
    out_ref, full_ref = refs[count:]
    cols = pieces[0].shape[0]
    for i, piece in enumerate(pieces):
        start = pl.multiple_of(place_ref[i] * cols, 16)
        full_ref[pl.ds(start, cols), :] = piece[...]
    order = cols * count
    where = {ab: n for n, ab in enumerate(lower_blocks(order // LANES))}
    wide = 2 * LANES
    for tile in range(order // wide):
        left = full_ref[tile * wide:, :]
        right = full_ref[tile * wide:(tile + 1) * wide, :]
        product = lax.dot_general(
            left, right, (((1,), (1,)), ((), ())), preferred_element_type=jnp.float32
        ) * scale
        for a in range(2 * tile, order // LANES):
            for b in range(2 * tile, min(2 * tile + 2, a + 1)):
                n = where[(a, b)]
                row = (a - 2 * tile) * LANES
                col = (b - 2 * tile) * LANES
                out_ref[n * LANES:(n + 1) * LANES, :] = product[row:row + LANES, col:col + LANES]


def gram(pieces, places, scale):
    cols, width = pieces[0].shape
    count = len(pieces)
    order = cols * count
    rows = len(lower_blocks(order // LANES)) * LANES
    return pl.pallas_call(
        functools.partial(gram_kernel, scale, count),
        out_shape=jax.ShapeDtypeStruct((rows, LANES), jnp.float32),
        in_specs=[pl.BlockSpec(memory_space=pltpu.SMEM)]
        + [pl.BlockSpec(memory_space=pltpu.VMEM)] * count,
        out_specs=pl.BlockSpec(memory_space=pltpu.VMEM),
        scratch_shapes=[pltpu.VMEM((order, width), jnp.bfloat16)],
        compiler_params=pltpu.CompilerParams(vmem_limit_bytes=40 * 2**20),
        cost_estimate=pl.CostEstimate(
            flops=2 * order * order * width,
            bytes_accessed=2 * order * width + 4 * rows * LANES,
            transcendentals=0,
        ),
        name="gram",
    )(places, *pieces)


def reduce_scatter(x, axis):
    n = lax.axis_size(axis)
    shares = x.reshape(n, x.shape[0] // n, LANES)
    return lax.all_to_all(shares, axis, split_axis=0, concat_axis=0, tiled=True).sum(axis=0)


def gather(x, axis):
    n = lax.axis_size(axis)
    copies = jnp.broadcast_to(x[None], (n, *x.shape))
    return lax.all_to_all(copies, axis, split_axis=0, concat_axis=0, tiled=True).reshape(
        n * x.shape[0], LANES
    )


def own_block(full_tri):
    order = full_tri.shape[0]
    row_count = order // lax.axis_size("dev")
    col_count = order // lax.axis_size("grp")
    row_start = lax.axis_index("dev") * row_count
    col_start = lax.axis_index("grp") * col_count
    return lax.dynamic_slice(full_tri, (row_start, col_start), (row_count, col_count))


def per_device(tensor_slab, mode_factor):
    depth, cols, slab_depth, species = tensor_slab.shape
    rank = mode_factor.shape[1]
    n_dev = lax.axis_size("dev")
    n_grp = lax.axis_size("grp")
    me = lax.axis_index("dev")
    slab = tensor_slab.transpose(1, 2, 3, 0).reshape(cols, slab_depth * species, depth)
    width = slab_depth * species // n_dev
    factor_pair = jnp.concatenate([mode_factor, mode_factor], axis=1)
    pieces, places = [], []
    for offset in list(range(n_dev // 2, n_dev)) + list(range(1, n_dev // 2)) + [0]:
        other = jnp.bitwise_xor(me, offset).astype(jnp.int32)
        piece = project(slab, factor_pair, rank, other, width)
        if offset:
            piece = lax.ppermute(piece, "dev", [(i, i ^ offset) for i in range(n_dev)])
        pieces.append(piece)
        places.append(other)
    row_total = rank * slab_depth * species * n_grp
    part = gram(pieces, jnp.stack(places), 1.0 / row_total)
    rows = part.shape[0]
    unit = 8 * n_dev * n_grp
    padded = jnp.pad(part, ((0, -rows % unit), (0, 0)))
    total = reduce_scatter(reduce_scatter(padded, "grp"), "dev")
    total = gather(gather(total, "dev"), "grp")
    order = cols * n_dev
    full = jnp.zeros((order, order), jnp.float32)
    for n, (a, b) in enumerate(lower_blocks(order // LANES)):
        block = total[n * LANES:(n + 1) * LANES]
        full = full.at[a * LANES:(a + 1) * LANES, b * LANES:(b + 1) * LANES].set(block)
    lower = lax.linalg.cholesky(full, symmetrize_input=False)
    return own_block(lower.T)


def solution(mesh):
    in_specs = (P(None, "dev", "grp", None), P())
    out_specs = P("dev", "grp")
    return jax.shard_map(
        per_device, mesh=mesh, in_specs=in_specs, out_specs=out_specs, check_vma=False
    )
```

time: 352 us -> 243 us (0.69)
  waiting for transfers between devices: 129 us -> 60.3 us
  blocking collectives: 100 us -> 37.4 us
  Pallas kernels: 0 us -> 43.3 us
  matrix products: 20.9 us -> 2.13 us
  starting transfers between devices: 0.01 us -> 14.6 us
  between operations: 16.1 us -> 2.88 us
    psum x1 -> x0, waiting for transfers between devices: 129 us -> none  [per_device(): gram_total = lax.psum(gram_local, ('grp', 'dev'))]
    all_to_all x1 -> x3, blocking collectives: 100 us -> 37.4 us  [the longest x2 27.4 us: reduce_scatter(): lax.all_to_all(shares, axis, split_axis=0, concat_axis=0, tiled=True)]
    ppermute x0 -> x7, waiting for transfers between devices: none -> 50.3 us  [per_device(): piece = lax.ppermute(piece, 'dev', [(i, i ^ offset) for i in range(n_dev)])]
    pallas_call x0 -> x9, Pallas kernels: none -> 43.3 us  [the longest x8 39.3 us: project(): pl.pallas_call(functools.partial(project_kernel, rank), out_shape=jax.Sha...]
    dot_general x2 -> x0, matrix products: 18.8 us -> none  [the longest x1 15.4 us: per_device(): lax.dot_general(mode_factor, flat_slab, (((0,), (0,)), ((), ())), preferr...]
    ppermute x0 -> x7, starting transfers between devices: none -> 10.9 us  [per_device(): piece = lax.ppermute(piece, 'dev', [(i, i ^ offset) for i in range(n_dev)])]
    all_to_all x0 -> x1, waiting for transfers between devices: none -> 10 us  [gather(): lax.all_to_all(copies, axis, split_axis=0, concat_axis=0, tiled=True)]
    all_to_all x0 -> x1, starting transfers between devices: none -> 3.66 us  [gather(): lax.all_to_all(copies, axis, split_axis=0, concat_axis=0, tiled=True)]
  transfers between devices with their start and end apart: 1 -> 8, of which waited for: 1 -> 5; matrix products, arithmetic and copies ran while one was open for 0% -> 0% of each run, Pallas kernels for 0% -> 14%
where the time goes in v1:
time: 243 us
  other arithmetic  78.9 us (32%)
  waiting for transfers between devices  60.3 us (25%)
  Pallas kernels  43.3 us (18%)
  blocking collectives  37.4 us (15%)
  starting transfers between devices  14.6 us (6%)
  local copies, waits for them, and re-layouts  3.09 us (1%)
  between operations  2.88 us (1%)
    another operation x14, other arithmetic, per_device(): lower = lax.linalg.cholesky(full, symmetrize_input=False)  78.6 us
    ppermute x7, waiting for transfers between devices, per_device(): piece = lax.ppermute(piece, 'dev', [(i, i ^ offset) for i in range(n_dev)])  50.3 us
    pallas_call x8, Pallas kernels, project(): pl.pallas_call(functools.partial(project_kernel, rank), out_shape=jax.Sha...  39.3 us
    all_to_all x2, blocking collectives, reduce_scatter(): lax.all_to_all(shares, axis, split_axis=0, concat_axis=0, tiled=True)  27.4 us
    ppermute x7, starting transfers between devices, per_device(): piece = lax.ppermute(piece, 'dev', [(i, i ^ offset) for i in range(n_dev)])  10.9 us
    all_to_all x1, waiting for transfers between devices, gather(): lax.all_to_all(copies, axis, split_axis=0, concat_axis=0, tiled=True)  10 us
    all_to_all x1, blocking collectives, gather(): lax.all_to_all(copies, axis, split_axis=0, concat_axis=0, tiled=True)  9.96 us
  transfers between devices with their start and end apart: 8, of which 5 were waited for; matrix products, arithmetic and copies ran while one was open for 0% of the time, Pallas kernels for 14%

profile of v1, /device:TPU:0, one launch (start us, length us, event | category | flops | bytes accessed | tf_op | source)
XLA Modules:
  0.0 242.5 jit_solution(16201688206241480524)
XLA Ops:
  0.0 1.0 copy.9
  1.1 4.8 %project.8 = bf16[64,4096]{1,0:T(8,128)(2,1)S(1)} custom-call(s32[1]{0:T(128)} %bitcast.dest_ref, bf16[64,512,512]{2,1,0:T(8,128)(2,1)} %bitcast.34, bf16[512,128]{1,0:T(8,128)(2,1)S(1)} %pad_maximum_fusion.factor_ref), custom_call_target="tpu_custom_call" | custom-call | flops 1073741824 | bytes 4718592 | tf_op jit(solution)/shard_map/project/pallas_call | solution.py:40
  5.9 4.1 %collective-permute-start = (bf16[64,4096]{1,0:T(8,128)(2,1)S(1)}, bf16[64,4096]{1,0:T(8,128)(2,1)}, u32[]{:S(2)}, u32[]{:S(2)}) collective-permute-start(bf16[64,4096]{1,0:T(8,128)(2,1)S(1)} %project.8), channel_id=1, source_target_pairs={{0,4},{1,5},{2,6},{3,7},{4,0},{5,1},{6,2},{7,3},{8,12},{9,13},{10,... | collective-permute-start | bytes 1572872 | tf_op jit(solution)/shard_map/ppermute | solution.py:141
  10.0 4.8 %project.9 = bf16[64,4096]{1,0:T(8,128)(2,1)S(1)} custom-call(s32[1]{0:T(128)} %bitcast.1.dest_ref, bf16[64,512,512]{2,1,0:T(8,128)(2,1)} %bitcast.35, bf16[512,128]{1,0:T(8,128)(2,1)S(1)} %pad_maximum_fusion.factor_ref), custom_call_target="tpu_custom_call" | custom-call | flops 1073741824 | bytes 4718592 | tf_op jit(solution)/shard_map/project/pallas_call | solution.py:40
  14.9 1.4 collective-permute-start.1
  16.2 4.8 %project.10 = bf16[64,4096]{1,0:T(8,128)(2,1)S(1)} custom-call(s32[1]{0:T(128)} %bitcast.2.dest_ref, bf16[64,512,512]{2,1,0:T(8,128)(2,1)} %bitcast.36, bf16[512,128]{1,0:T(8,128)(2,1)S(1)} %pad_maximum_fusion.factor_ref), custom_call_target="tpu_custom_call" | custom-call | flops 1073741824 | bytes 4718592 | tf_op jit(solution)/shard_map/project/pallas_call | solution.py:40
  21.1 3.6 %collective-permute-start.2 = (bf16[64,4096]{1,0:T(8,128)(2,1)S(1)}, bf16[64,4096]{1,0:T(8,128)(2,1)}, u32[]{:S(2)}, u32[]{:S(2)}) collective-permute-start(bf16[64,4096]{1,0:T(8,128)(2,1)S(1)} %project.10), channel_id=1, source_target_pairs={{0,6},{1,7},{2,4},{3,5},{4,2},{5,3},{6,0},{7,1},{8,14},{9,15},{10,... | collective-permute-start | bytes 1572872 | tf_op jit(solution)/shard_map/ppermute | solution.py:141
  24.7 4.8 %project.11 = bf16[64,4096]{1,0:T(8,128)(2,1)S(1)} custom-call(s32[1]{0:T(128)} %bitcast.3.dest_ref, bf16[64,512,512]{2,1,0:T(8,128)(2,1)} %bitcast.37, bf16[512,128]{1,0:T(8,128)(2,1)S(1)} %pad_maximum_fusion.factor_ref), custom_call_target="tpu_custom_call" | custom-call | flops 1073741824 | bytes 4718592 | tf_op jit(solution)/shard_map/project/pallas_call | solution.py:40
  29.6 4.8 %project.12 = bf16[64,4096]{1,0:T(8,128)(2,1)S(1)} custom-call(s32[1]{0:T(128)} %bitcast.4.dest_ref, bf16[64,512,512]{2,1,0:T(8,128)(2,1)} %bitcast.38, bf16[512,128]{1,0:T(8,128)(2,1)S(1)} %pad_maximum_fusion.factor_ref), custom_call_target="tpu_custom_call" | custom-call | flops 1073741824 | bytes 4718592 | tf_op jit(solution)/shard_map/project/pallas_call | solution.py:40
  34.5 1.7 collective-permute-start.4
  36.2 4.8 %project.14 = bf16[64,4096]{1,0:T(8,128)(2,1)S(1)} custom-call(s32[1]{0:T(128)} %bitcast.6.dest_ref, bf16[64,512,512]{2,1,0:T(8,128)(2,1)} %bitcast.39, bf16[512,128]{1,0:T(8,128)(2,1)S(1)} %pad_maximum_fusion.factor_ref), custom_call_target="tpu_custom_call" | custom-call | flops 1073741824 | bytes 4718592 | tf_op jit(solution)/shard_map/project/pallas_call | solution.py:40
  41.0 5.5 %project.13 = bf16[64,4096]{1,0:T(8,128)(2,1)} custom-call(s32[1]{0:T(128)} %bitcast.5.dest_ref, bf16[64,512,512]{2,1,0:T(8,128)(2,1)} %bitcast.40, bf16[512,128]{1,0:T(8,128)(2,1)S(1)} %pad_maximum_fusion.factor_ref), custom_call_target="tpu_custom_call" | custom-call | flops 1073741824 | bytes 4718592 | tf_op jit(solution)/shard_map/project/pallas_call | solution.py:40
  46.6 21.3 %collective-permute-done.refs_0_ = bf16[64,4096]{1,0:T(8,128)(2,1)} collective-permute-done((bf16[64,4096]{1,0:T(8,128)(2,1)S(1)}, bf16[64,4096]{1,0:T(8,128)(2,1)}, u32[]{:S(2)}, u32[]{:S(2)}) %collective-permute-start) | collective-permute-done | bytes 524320 | tf_op jit(solution)/shard_map/ppermute | solution.py:141
  67.9 12.6 %collective-permute-done.1.refs_1_ = bf16[64,4096]{1,0:T(8,128)(2,1)} collective-permute-done((bf16[64,4096]{1,0:T(8,128)(2,1)S(1)}, bf16[64,4096]{1,0:T(8,128)(2,1)}, u32[]{:S(2)}, u32[]{:S(2)}) %collective-permute-start.1) | collective-permute-done | bytes 524320 | tf_op jit(solution)/shard_map/ppermute | solution.py:141
  80.6 4.8 %project.15.refs_7_ = bf16[64,4096]{1,0:T(8,128)(2,1)S(1)} custom-call(s32[1]{0:T(128)} %bitcast.7.dest_ref, bf16[64,512,512]{2,1,0:T(8,128)(2,1)} %bitcast.41, bf16[512,128]{1,0:T(8,128)(2,1)S(1)} %pad_maximum_fusion.factor_ref), custom_call_target="tpu_custom_call" | custom-call | flops 1073741824 | bytes 4718592 | tf_op jit(solution)/shard_map/project/pallas_call | solution.py:40
  85.4 4.1 %collective-permute-done.5.refs_5_ = bf16[64,4096]{1,0:T(8,128)(2,1)S(1)} collective-permute-done((bf16[64,4096]{1,0:T(8,128)(2,1)}, bf16[64,4096]{1,0:T(8,128)(2,1)S(1)}, u32[]{:S(2)}, u32[]{:S(2)}) %collective-permute-start.5) | collective-permute-done | bytes 524320 | tf_op jit(solution)/shard_map/ppermute | solution.py:141
  89.5 12.3 %collective-permute-done.6.refs_6_ = bf16[64,4096]{1,0:T(8,128)(2,1)} collective-permute-done((bf16[64,4096]{1,0:T(8,128)(2,1)S(1)}, bf16[64,4096]{1,0:T(8,128)(2,1)}, u32[]{:S(2)}, u32[]{:S(2)}) %collective-permute-start.6) | collective-permute-done | bytes 524320 | tf_op jit(solution)/shard_map/ppermute | solution.py:141
  101.8 3.9 %gram.1 = f32[1280,128]{1,0:T(8,128)S(1)} custom-call(s32[8]{0:T(128)S(1)} %stack.35.place_ref, bf16[64,4096]{1,0:T(8,128)(2,1)} %collective-permute-done.refs_0_, bf16[64,4096]{1,0:T(8,128)(2,1)} %collective-permute-done.1.refs_1_, bf16[64,4096]{1,0:T(8,128)(2,1)} %collective-permute-done.2.refs_2_, bf16[64,4096]{1,0:T(8,128)(2,1)} %collective-permute-done.3.refs_3_, ...), custom_call_target="tpu_custom_call" | custom-call | flops 2147483648 | bytes 4849664 | tf_op jit(solution)/shard_map/gram/pallas_call | solution.py:87
  105.7 12.8 %all_to_all.20 = f32[4,320,128]{2,1,0:T(8,128)S(1)} all-to-all(f32[4,320,128]{2,1,0:T(8,128)S(1)} %bitcast.33), channel_id=1, replica_groups=mesh['grp'=4,'dev'=8] {'grp'}, dimensions={0} | all-to-all | bytes 1310720 | tf_op jit(solution)/shard_map/all_to_all | solution.py:107
  118.6 14.6 %all_to_all.21 = f32[8,40,128]{2,1,0:T(8,128)S(1)} all-to-all(f32[8,40,128]{2,1,0:T(8,128)S(1)} %bitcast.52), channel_id=1, replica_groups=mesh['grp'=4,'dev'=8] {'dev'}, dimensions={0} | all-to-all | bytes 327680 | tf_op jit(solution)/shard_map/all_to_all | solution.py:107
  133.2 10.0 %all_to_all.22 = f32[8,40,128]{2,1,0:T(8,128)S(1)} all-to-all(f32[8,40,128]{2,1,0:T(8,128)S(1)} %broadcast_in_dim.6), channel_id=1, replica_groups=mesh['grp'=4,'dev'=8] {'dev'}, dimensions={0} | all-to-all | bytes 327680 | tf_op jit(solution)/shard_map/all_to_all | solution.py:113
  143.2 0.9 broadcast_in_dim.15
  144.1 3.7 %all-to-all-start.3 = ((f32[4,320,128]{2,1,0:T(8,128)}), f32[4,320,128]{2,1,0:T(8,128)S(1)}, u32[]{:S(2)}, u32[]{:S(2)}) async-start(f32[4,320,128]{2,1,0:T(8,128)} %broadcast_in_dim.15), calls=%async_computation.3 | async-start | bytes 1310720 | tf_op jit(solution)/shard_map/all_to_all | solution.py:113
  147.7 10.0 %all-to-all-done.3 = f32[4,320,128]{2,1,0:T(8,128)S(1)} async-done(((f32[4,320,128]{2,1,0:T(8,128)}), f32[4,320,128]{2,1,0:T(8,128)S(1)}, u32[]{:S(2)}, u32[]{:S(2)}) %all-to-all-start.3) | async-done | bytes 655392 | tf_op jit(solution)/shard_map/all_to_all | solution.py:113
  158.0 11.7 %cholesky.101 = f32[128,128]{1,0:T(8,128)S(1)} custom-call(f32[128,128]{1,0:T(8,128)S(1)} %cholesky.257), custom_call_target="Cholesky" | custom-call | tf_op jit(solution)/shard_map/cholesky | solution.py:156
  169.8 9.8 %custom-call.20 = f32[1,128,128]{1,2,0:T(8,128)S(1)} custom-call(f32[1,128,128]{2,1,0:T(8,128)S(1)} %get-tuple-element.134), custom_call_target="InvertDiagBlocksLowerTriangular" | custom-call | tf_op jit(solution)/shard_map/cholesky | solution.py:156
  180.8 11.7 %cholesky.210 = f32[128,128]{1,0:T(8,128)S(1)} custom-call(f32[128,128]{1,0:T(8,128)S(1)} %cholesky.261), custom_call_target="Cholesky" | custom-call | tf_op jit(solution)/shard_map/cholesky | solution.py:156
  192.6 10.0 %custom-call.21 = f32[1,128,128]{1,2,0:T(8,128)S(1)} custom-call(f32[1,128,128]{2,1,0:T(8,128)S(1)} %get-tuple-element.131), custom_call_target="InvertDiagBlocksLowerTriangular" | custom-call | tf_op jit(solution)/shard_map/cholesky | solution.py:156
  203.2 11.7 %cholesky.231 = f32[128,128]{1,0:T(8,128)S(1)} custom-call(f32[128,128]{1,0:T(8,128)S(1)} %cholesky.266), custom_call_target="Cholesky" | custom-call | tf_op jit(solution)/shard_map/cholesky | solution.py:156
  215.0 0.7 compare_reduce_fusion.1
  215.7 9.8 %custom-call.22 = f32[1,128,128]{1,2,0:T(8,128)S(1)} custom-call(f32[1,128,128]{2,1,0:T(8,128)S(1)} %get-tuple-element.128), custom_call_target="InvertDiagBlocksLowerTriangular" | custom-call | tf_op jit(solution)/shard_map/cholesky | solution.py:156
  226.1 11.7 %cholesky.247 = f32[128,128]{1,0:T(8,128)S(1)} custom-call(f32[128,128]{1,0:T(8,128)S(1)} %convolution_subtract_fusion.2), custom_call_target="Cholesky" | custom-call | tf_op jit(solution)/shard_map/cholesky | solution.py:156
  (41 shorter events, 5.2 us)
Async XLA Ops:
  5.9 61.9 %collective-permute-start = (bf16[64,4096]{1,0:T(8,128)(2,1)S(1)}, bf16[64,4096]{1,0:T(8,128)(2,1)}, u32[]{:S(2)}, u32[]{:S(2)}) collective-permute-start(bf16[64,4096]{1,0:T(8,128)(2,1)S(1)} %project.8), channel_id=1, source_target_pairs={{0,4},{1,5},{2,6},{3,7},{4,0},{5,1},{6,2},{7,3},{8,12},{9,13},{10,... | collective-permute-start | bytes 1572872 | tf_op jit(solution)/shard_map/ppermute | solution.py:141
  14.9 65.6 %collective-permute-start.1 = (bf16[64,4096]{1,0:T(8,128)(2,1)S(1)}, bf16[64,4096]{1,0:T(8,128)(2,1)}, u32[]{:S(2)}, u32[]{:S(2)}) collective-permute-start(bf16[64,4096]{1,0:T(8,128)(2,1)S(1)} %project.9), channel_id=1, source_target_pairs={{0,5},{1,4},{2,7},{3,6},{4,1},{5,0},{6,3},{7,2},{8,13},{9,12},{10,... | collective-permute-start | bytes 1572872 | tf_op jit(solution)/shard_map/ppermute | solution.py:141
  21.1 64.3 %collective-permute-start.2 = (bf16[64,4096]{1,0:T(8,128)(2,1)S(1)}, bf16[64,4096]{1,0:T(8,128)(2,1)}, u32[]{:S(2)}, u32[]{:S(2)}) collective-permute-start(bf16[64,4096]{1,0:T(8,128)(2,1)S(1)} %project.10), channel_id=1, source_target_pairs={{0,6},{1,7},{2,4},{3,5},{4,2},{5,3},{6,0},{7,1},{8,14},{9,15},{10,... | collective-permute-start | bytes 1572872 | tf_op jit(solution)/shard_map/ppermute | solution.py:141
  29.5 55.9 %collective-permute-start.3 = (bf16[64,4096]{1,0:T(8,128)(2,1)S(1)}, bf16[64,4096]{1,0:T(8,128)(2,1)}, u32[]{:S(2)}, u32[]{:S(2)}) collective-permute-start(bf16[64,4096]{1,0:T(8,128)(2,1)S(1)} %project.11), channel_id=1, source_target_pairs={{0,7},{1,6},{2,5},{3,4},{4,3},{5,2},{6,1},{7,0},{8,15},{9,14},{10,... | collective-permute-start | bytes 1572872 | tf_op jit(solution)/shard_map/ppermute | solution.py:141
  34.5 50.9 %collective-permute-start.4 = (bf16[64,4096]{1,0:T(8,128)(2,1)S(1)}, bf16[64,4096]{1,0:T(8,128)(2,1)}, u32[]{:S(2)}, u32[]{:S(2)}) collective-permute-start(bf16[64,4096]{1,0:T(8,128)(2,1)S(1)} %project.12), channel_id=1, source_target_pairs={{0,1},{1,0},{2,3},{3,2},{4,5},{5,4},{6,7},{7,6},{8,9},{9,8},{10,11... | collective-permute-start | bytes 1572872 | tf_op jit(solution)/shard_map/ppermute | solution.py:141
  67.9 21.6 %collective-permute-start.5 = (bf16[64,4096]{1,0:T(8,128)(2,1)}, bf16[64,4096]{1,0:T(8,128)(2,1)S(1)}, u32[]{:S(2)}, u32[]{:S(2)}) collective-permute-start(bf16[64,4096]{1,0:T(8,128)(2,1)} %project.13), channel_id=1, source_target_pairs={{0,2},{1,3},{2,0},{3,1},{4,6},{5,7},{6,4},{7,5},{8,10},{9,11},{10,... | collective-permute-start | bytes 1572872 | tf_op jit(solution)/shard_map/ppermute | solution.py:141
  80.5 21.3 %collective-permute-start.6 = (bf16[64,4096]{1,0:T(8,128)(2,1)S(1)}, bf16[64,4096]{1,0:T(8,128)(2,1)}, u32[]{:S(2)}, u32[]{:S(2)}) collective-permute-start(bf16[64,4096]{1,0:T(8,128)(2,1)S(1)} %project.14), channel_id=1, source_target_pairs={{0,3},{1,2},{2,1},{3,0},{4,7},{5,6},{6,5},{7,4},{8,11},{9,10},{10,... | collective-permute-start | bytes 1572872 | tf_op jit(solution)/shard_map/ppermute | solution.py:141
  144.1 13.7 %all-to-all-start.3 = ((f32[4,320,128]{2,1,0:T(8,128)}), f32[4,320,128]{2,1,0:T(8,128)S(1)}, u32[]{:S(2)}, u32[]{:S(2)}) async-start(f32[4,320,128]{2,1,0:T(8,128)} %broadcast_in_dim.15), calls=%async_computation.3 | async-start | bytes 1310720 | tf_op jit(solution)/shard_map/all_to_all | solution.py:113

commit v2 on v1

--- a/solution.py
+++ b/solution.py
@@ -51,8 +51,8 @@
     )(dest.reshape(1), slab, factor_pair)
 
 
-def lower_blocks(count):
-    return [(a, b) for a in range(count) for b in range(a + 1)]
+def upper_blocks(count):
+    return [(a, b) for a in range(count) for b in range(a, count)]
 
 
 def gram_kernel(scale, count, place_ref, *refs):
@@ -63,27 +63,26 @@
         start = pl.multiple_of(place_ref[i] * cols, 16)
         full_ref[pl.ds(start, cols), :] = piece[...]
     order = cols * count
-    where = {ab: n for n, ab in enumerate(lower_blocks(order // LANES))}
+    where = {ab: n for n, ab in enumerate(upper_blocks(order // LANES))}
     wide = 2 * LANES
     for tile in range(order // wide):
-        left = full_ref[tile * wide:, :]
+        left = full_ref[:(tile + 1) * wide, :]
         right = full_ref[tile * wide:(tile + 1) * wide, :]
         product = lax.dot_general(
             left, right, (((1,), (1,)), ((), ())), preferred_element_type=jnp.float32
         ) * scale
-        for a in range(2 * tile, order // LANES):
-            for b in range(2 * tile, min(2 * tile + 2, a + 1)):
+        for b in range(2 * tile, 2 * tile + 2):
+            for a in range(b + 1):
                 n = where[(a, b)]
-                row = (a - 2 * tile) * LANES
                 col = (b - 2 * tile) * LANES
-                out_ref[n * LANES:(n + 1) * LANES, :] = product[row:row + LANES, col:col + LANES]
+                out_ref[n * LANES:(n + 1) * LANES, :] = product[a * LANES:(a + 1) * LANES, col:col + LANES]
 
 
 def gram(pieces, places, scale):
     cols, width = pieces[0].shape
     count = len(pieces)
     order = cols * count
-    rows = len(lower_blocks(order // LANES)) * LANES
+    rows = len(upper_blocks(order // LANES)) * LANES
     return pl.pallas_call(
         functools.partial(gram_kernel, scale, count),
         out_shape=jax.ShapeDtypeStruct((rows, LANES), jnp.float32),
@@ -115,13 +114,119 @@
     )
 
 
-def own_block(full_tri):
-    order = full_tri.shape[0]
+def spread_lane(rows, lane):
+    return jnp.broadcast_to(rows[:, lane:lane + 1], rows.shape)
+
+
+def spread_row(rows, row):
+    return jnp.broadcast_to(rows[row:row + 1, :], rows.shape)
+
+
+def factor_block(block, step):
+    lane = lax.broadcasted_iota(jnp.int32, (step, LANES), 1)
+    row = lax.broadcasted_iota(jnp.int32, (step, LANES), 0)
+    rows = [block[i * step:(i + 1) * step, :] for i in range(LANES // step)]
+    tri_rows, inv_rows = [], []
+    for t, head in enumerate(rows):
+        first = t * step
+        inside = (lane >= first) & (lane < first + step)
+        spread = [spread_lane(head, first + b) for b in range(step)]
+        s = {(a, b): spread_row(spread[b], a) for a in range(step) for b in range(a, step)}
+        r, inv_diag = {}, []
+        for k in range(step):
+            inv = lax.rsqrt(s[k, k])
+            inv_diag.append(inv)
+            for b in range(k, step):
+                r[k, b] = s[k, b] * inv
+            for a in range(k + 1, step):
+                for b in range(a, step):
+                    s[a, b] = s[a, b] - r[k, a] * r[k, b]
+        tri, mix = [], []
+        for k in range(step):
+            raw = spread_row(head, k)
+            x = raw
+            y = jnp.where(inside, jnp.where(lane == first + k, 1.0, 0.0), raw)
+            for m in range(k):
+                x = x - r[m, k] * tri[m]
+                y = y - r[m, k] * mix[m]
+            tri.append(x * inv_diag[k])
+            mix.append(y * inv_diag[k])
+        tri_out, mix_out = tri[0], mix[0]
+        for k in range(1, step):
+            tri_out = jnp.where(row == k, tri[k], tri_out)
+            mix_out = jnp.where(row == k, mix[k], mix_out)
+        tri_rows.append(jnp.where(lane >= row + first, tri_out, 0.0))
+        inv_rows.append(jnp.where(lane <= row + first, mix_out, 0.0))
+        for i in range(t + 1, LANES // step):
+            col, held = [], jnp.where(inside, 0.0, rows[i])
+            for k in range(step):
+                c = spread_lane(rows[i], first + k)
+                for m in range(k):
+                    c = c - r[m, k] * col[m]
+                col.append(c * inv_diag[k])
+                held = held - col[k] * mix[k]
+            rows[i] = held
+    return tri_rows, inv_rows
+
+
+def triangle_kernel(count, place_ref, blocks_ref, out_ref, work_ref, tri_ref, inv_ref):
+    step = 8
+    high = lax.Precision.HIGHEST
+    where = {ab: n for n, ab in enumerate(upper_blocks(count))}
+
+    def at(a, b):
+        return pl.ds(where[a, b] * LANES, LANES)
+
+    work_ref[...] = blocks_ref[:len(where) * LANES, :]
+    tri_ref[...] = jnp.zeros_like(tri_ref)
+    for p in range(count):
+        tri_rows, inv_rows = factor_block(work_ref[at(p, p), :], step)
+        for i in range(LANES // step):
+            tri_ref[p * LANES + i * step:p * LANES + (i + 1) * step, p * LANES:(p + 1) * LANES] = tri_rows[i]
+            inv_ref[i * step:(i + 1) * step, :] = inv_rows[i]
+        for q in range(p + 1, count):
+            tri_ref[p * LANES:(p + 1) * LANES, q * LANES:(q + 1) * LANES] = jnp.dot(
+                inv_ref[...], work_ref[at(p, q), :], precision=high, preferred_element_type=jnp.float32
+            )
+        for a in range(p + 1, count):
+            for b in range(a, count):
+                work_ref[at(a, b), :] -= lax.dot_general(
+                    tri_ref[p * LANES:(p + 1) * LANES, a * LANES:(a + 1) * LANES],
+                    tri_ref[p * LANES:(p + 1) * LANES, b * LANES:(b + 1) * LANES],
+                    (((0,), (0,)), ((), ())), precision=high, preferred_element_type=jnp.float32,
+                )
+    out_rows = out_ref.shape[0]
+    row = pl.multiple_of(place_ref[0] * out_rows, 8)
+    col = pl.multiple_of(place_ref[1] * LANES, LANES)
+    out_ref[...] = tri_ref[pl.ds(row, out_rows), pl.ds(col, LANES)]
+
+
+def own_triangle(blocks, order):
     row_count = order // lax.axis_size("dev")
     col_count = order // lax.axis_size("grp")
-    row_start = lax.axis_index("dev") * row_count
-    col_start = lax.axis_index("grp") * col_count
-    return lax.dynamic_slice(full_tri, (row_start, col_start), (row_count, col_count))
+    grp = lax.axis_index("grp")
+    place = jnp.stack([lax.axis_index("dev"), grp * col_count // LANES]).astype(jnp.int32)
+    count = order // LANES
+    rows = len(upper_blocks(count)) * LANES
+    out = pl.pallas_call(
+        functools.partial(triangle_kernel, count),
+        out_shape=jax.ShapeDtypeStruct((row_count, LANES), jnp.float32),
+        in_specs=[pl.BlockSpec(memory_space=pltpu.SMEM), pl.BlockSpec(memory_space=pltpu.VMEM)],
+        out_specs=pl.BlockSpec(memory_space=pltpu.VMEM),
+        scratch_shapes=[
+            pltpu.VMEM((rows, LANES), jnp.float32),
+            pltpu.VMEM((order, order), jnp.float32),
+            pltpu.VMEM((LANES, LANES), jnp.float32),
+        ],
+        compiler_params=pltpu.CompilerParams(vmem_limit_bytes=32 * 2**20),
+        cost_estimate=pl.CostEstimate(
+            flops=order**3, bytes_accessed=4 * order * order, transcendentals=order
+        ),
+        name="triangle",
+    )(place, blocks)
+    if col_count == LANES:
+        return out
+    return lax.dynamic_slice(out, (0, grp * col_count % LANES), (row_count, col_count))
 
 
 def per_device(tensor_slab, mode_factor):
@@ -134,7 +239,10 @@
     width = slab_depth * species // n_dev
     factor_pair = jnp.concatenate([mode_factor, mode_factor], axis=1)
     pieces, places = [], []
-    for offset in list(range(n_dev // 2, n_dev)) + list(range(1, n_dev // 2)) + [0]:
+    half = n_dev // 2
+    near, far = list(range(1, half)), list(range(half, n_dev))
+    order = far[:1] + near[:1] + far[1:2] + near[1:2] + far[2:] + near[2:] + [0]
+    for offset in order:
         other = jnp.bitwise_xor(me, offset).astype(jnp.int32)
         piece = project(slab, factor_pair, rank, other, width)
         if offset:
@@ -148,13 +256,7 @@
     padded = jnp.pad(part, ((0, -rows % unit), (0, 0)))
     total = reduce_scatter(reduce_scatter(padded, "grp"), "dev")
     total = gather(gather(total, "dev"), "grp")
-    order = cols * n_dev
-    full = jnp.zeros((order, order), jnp.float32)
-    for n, (a, b) in enumerate(lower_blocks(order // LANES)):
-        block = total[n * LANES:(n + 1) * LANES]
-        full = full.at[a * LANES:(a + 1) * LANES, b * LANES:(b + 1) * LANES].set(block)
-    lower = lax.linalg.cholesky(full, symmetrize_input=False)
-    return own_block(lower.T)
+    return own_triangle(total, cols * n_dev)
 
 
 def solution(mesh):

time: 243 us -> 175 us (0.72)
  other arithmetic: 78.9 us -> 0.24 us
  Pallas kernels: 43.3 us -> 61.7 us
  waiting for transfers between devices: 60.3 us -> 48.4 us
  blocking collectives: 37.4 us -> 42.4 us
  starting transfers between devices: 14.6 us -> 18.8 us
  between operations: 2.88 us -> 0.14 us
    another operation x14 -> x1, other arithmetic: 78.6 us -> 0.08 us  [own_triangle(): jnp.stack([lax.axis_index('dev'), grp * col_count // LANES])]
    pallas_call x0 -> x1, Pallas kernels: none -> 18.3 us  [own_triangle(): pl.pallas_call(functools.partial(triangle_kernel, count), out_shape=jax.S...]
    ppermute x7, waiting for transfers between devices: 50.3 us -> 38.5 us  [per_device(): piece = lax.ppermute(piece, 'dev', [(i, i ^ offset) for i in range(n_dev)])]
    all_to_all x2, blocking collectives: 27.4 us -> 32.4 us  [reduce_scatter(): lax.all_to_all(shares, axis, split_axis=0, concat_axis=0, tiled=True)]
    ppermute x7, starting transfers between devices: 10.9 us -> 15.2 us  [per_device(): piece = lax.ppermute(piece, 'dev', [(i, i ^ offset) for i in range(n_dev)])]
  transfers between devices with their start and end apart: 8 -> 8, of which waited for: 5 -> 5; matrix products, arithmetic and copies ran while one was open for 0% -> 0% of each run, Pallas kernels for 14% -> 19%
where the time goes in v2:
time: 175 us; the launch traced here: 174 us
  Pallas kernels  61.7 us (35%)
  waiting for transfers between devices  48.4 us (28%)
  blocking collectives  42.4 us (24%)
  starting transfers between devices  18.8 us (11%)
  local copies, waits for them, and re-layouts  1.93 us (1%)
    pallas_call x8, Pallas kernels, project(): pl.pallas_call(functools.partial(project_kernel, rank), out_shape=jax.Sha...  39.3 us
    ppermute x7, waiting for transfers between devices, per_device(): piece = lax.ppermute(piece, 'dev', [(i, i ^ offset) for i in range(n_dev)])  38.5 us
    all_to_all x2, blocking collectives, reduce_scatter(): lax.all_to_all(shares, axis, split_axis=0, concat_axis=0, tiled=True)  32.4 us
    pallas_call x1, Pallas kernels, own_triangle(): pl.pallas_call(functools.partial(triangle_kernel, count), out_shape=jax.S...  18.3 us
    ppermute x7, starting transfers between devices, per_device(): piece = lax.ppermute(piece, 'dev', [(i, i ^ offset) for i in range(n_dev)])  15.2 us
    all_to_all x1, blocking collectives, gather(): lax.all_to_all(copies, axis, split_axis=0, concat_axis=0, tiled=True)  9.96 us
    all_to_all x1, waiting for transfers between devices, gather(): lax.all_to_all(copies, axis, split_axis=0, concat_axis=0, tiled=True)  9.94 us
    pallas_call x1, Pallas kernels, gram(): pl.pallas_call(functools.partial(gram_kernel, scale, count), out_shape=ja...  4.09 us
  transfers between devices with their start and end apart: 8, of which 5 were waited for; matrix products, arithmetic and copies ran while one was open for 0% of the time, Pallas kernels for 19%

profile of v2, /device:TPU:0, one launch (start us, length us, event | category | flops | bytes accessed | tf_op | source)
XLA Modules:
  0.0 173.6 jit_solution(9607729203145566403)
XLA Ops:
  0.0 1.0 copy.5
  1.0 0.1 pad_maximum_fusion.factor_ref
  1.1 5.5 %project.8 = bf16[64,4096]{1,0:T(8,128)(2,1)} custom-call(s32[1]{0:T(128)} %bitcast.2.dest_ref, bf16[64,512,512]{2,1,0:T(8,128)(2,1)} %bitcast.18, bf16[512,128]{1,0:T(8,128)(2,1)S(1)} %pad_maximum_fusion.factor_ref), custom_call_target="tpu_custom_call" | custom-call | flops 1073741824 | bytes 4718592 | tf_op jit(solution)/shard_map/project/pallas_call | solution.py:40
  6.6 4.0 %collective-permute-start = (bf16[64,4096]{1,0:T(8,128)(2,1)}, bf16[64,4096]{1,0:T(8,128)(2,1)}, u32[]{:S(2)}, u32[]{:S(2)}) collective-permute-start(bf16[64,4096]{1,0:T(8,128)(2,1)} %project.8), channel_id=1, source_target_pairs={{0,4},{1,5},{2,6},{3,7},{4,0},{5,1},{6,2},{7,3},{8,12},{9,13},{10,... | collective-permute-start | bytes 1572872 | tf_op jit(solution)/shard_map/ppermute | solution.py:249
  10.6 4.8 %project.9 = bf16[64,4096]{1,0:T(8,128)(2,1)S(1)} custom-call(s32[1]{0:T(128)} %bitcast.3.dest_ref, bf16[64,512,512]{2,1,0:T(8,128)(2,1)} %bitcast.19, bf16[512,128]{1,0:T(8,128)(2,1)S(1)} %pad_maximum_fusion.factor_ref), custom_call_target="tpu_custom_call" | custom-call | flops 1073741824 | bytes 4718592 | tf_op jit(solution)/shard_map/project/pallas_call | solution.py:40
  15.5 1.6 collective-permute-start.1
  17.1 4.8 %project.10 = bf16[64,4096]{1,0:T(8,128)(2,1)S(1)} custom-call(s32[1]{0:T(128)} %bitcast.4.dest_ref, bf16[64,512,512]{2,1,0:T(8,128)(2,1)} %bitcast.20, bf16[512,128]{1,0:T(8,128)(2,1)S(1)} %pad_maximum_fusion.factor_ref), custom_call_target="tpu_custom_call" | custom-call | flops 1073741824 | bytes 4718592 | tf_op jit(solution)/shard_map/project/pallas_call | solution.py:40
  21.9 0.1 collective-permute-start.2
  22.0 4.8 %project.11 = bf16[64,4096]{1,0:T(8,128)(2,1)S(1)} custom-call(s32[1]{0:T(128)} %bitcast.5.dest_ref, bf16[64,512,512]{2,1,0:T(8,128)(2,1)} %bitcast.21, bf16[512,128]{1,0:T(8,128)(2,1)S(1)} %pad_maximum_fusion.factor_ref), custom_call_target="tpu_custom_call" | custom-call | flops 1073741824 | bytes 4718592 | tf_op jit(solution)/shard_map/project/pallas_call | solution.py:40
  26.8 1.9 %collective-permute-start.3 = (bf16[64,4096]{1,0:T(8,128)(2,1)S(1)}, bf16[64,4096]{1,0:T(8,128)(2,1)}, u32[]{:S(2)}, u32[]{:S(2)}) collective-permute-start(bf16[64,4096]{1,0:T(8,128)(2,1)S(1)} %project.11), channel_id=1, source_target_pairs={{0,2},{1,3},{2,0},{3,1},{4,6},{5,7},{6,4},{7,5},{8,10},{9,11},{10,... | collective-permute-start | bytes 1572872 | tf_op jit(solution)/shard_map/ppermute | solution.py:249
  28.7 4.8 %project.12 = bf16[64,4096]{1,0:T(8,128)(2,1)S(1)} custom-call(s32[1]{0:T(128)} %bitcast.6.dest_ref, bf16[64,512,512]{2,1,0:T(8,128)(2,1)} %bitcast.22, bf16[512,128]{1,0:T(8,128)(2,1)S(1)} %pad_maximum_fusion.factor_ref), custom_call_target="tpu_custom_call" | custom-call | flops 1073741824 | bytes 4718592 | tf_op jit(solution)/shard_map/project/pallas_call | solution.py:40
  33.5 2.5 %collective-permute-start.4 = (bf16[64,4096]{1,0:T(8,128)(2,1)S(1)}, bf16[64,4096]{1,0:T(8,128)(2,1)}, u32[]{:S(2)}, u32[]{:S(2)}) collective-permute-start(bf16[64,4096]{1,0:T(8,128)(2,1)S(1)} %project.12), channel_id=1, source_target_pairs={{0,6},{1,7},{2,4},{3,5},{4,2},{5,3},{6,0},{7,1},{8,14},{9,15},{10,... | collective-permute-start | bytes 1572872 | tf_op jit(solution)/shard_map/ppermute | solution.py:249
  36.1 4.8 %project.14 = bf16[64,4096]{1,0:T(8,128)(2,1)S(1)} custom-call(s32[1]{0:T(128)} %bitcast.8.dest_ref, bf16[64,512,512]{2,1,0:T(8,128)(2,1)} %bitcast.23, bf16[512,128]{1,0:T(8,128)(2,1)S(1)} %pad_maximum_fusion.factor_ref), custom_call_target="tpu_custom_call" | custom-call | flops 1073741824 | bytes 4718592 | tf_op jit(solution)/shard_map/project/pallas_call | solution.py:40
  40.9 4.8 %project.13 = bf16[64,4096]{1,0:T(8,128)(2,1)S(1)} custom-call(s32[1]{0:T(128)} %bitcast.7.dest_ref, bf16[64,512,512]{2,1,0:T(8,128)(2,1)} %bitcast.24, bf16[512,128]{1,0:T(8,128)(2,1)S(1)} %pad_maximum_fusion.factor_ref), custom_call_target="tpu_custom_call" | custom-call | flops 1073741824 | bytes 4718592 | tf_op jit(solution)/shard_map/project/pallas_call | solution.py:40
  45.8 0.5 collective-permute-done.refs_0_
  46.3 5.1 %collective-permute-start.5 = (bf16[64,4096]{1,0:T(8,128)(2,1)S(1)}, bf16[64,4096]{1,0:T(8,128)(2,1)}, u32[]{:S(2)}, u32[]{:S(2)}) collective-permute-start(bf16[64,4096]{1,0:T(8,128)(2,1)S(1)} %project.13), channel_id=1, source_target_pairs={{0,7},{1,6},{2,5},{3,4},{4,3},{5,2},{6,1},{7,0},{8,15},{9,14},{10,... | collective-permute-start | bytes 1572872 | tf_op jit(solution)/shard_map/ppermute | solution.py:249
  51.4 0.0 collective-permute-done.1.refs_1_
  51.4 0.1 stack.44.place_ref
  51.4 4.8 %project.15.refs_7_ = bf16[64,4096]{1,0:T(8,128)(2,1)S(1)} custom-call(s32[1]{0:T(128)} %bitcast.dest_ref, bf16[64,512,512]{2,1,0:T(8,128)(2,1)} %bitcast.25, bf16[512,128]{1,0:T(8,128)(2,1)S(1)} %pad_maximum_fusion.factor_ref), custom_call_target="tpu_custom_call" | custom-call | flops 1073741824 | bytes 4718592 | tf_op jit(solution)/shard_map/project/pallas_call | solution.py:40
  56.3 25.0 %collective-permute-done.2.refs_2_ = bf16[64,4096]{1,0:T(8,128)(2,1)} collective-permute-done((bf16[64,4096]{1,0:T(8,128)(2,1)S(1)}, bf16[64,4096]{1,0:T(8,128)(2,1)}, u32[]{:S(2)}, u32[]{:S(2)}) %collective-permute-start.2) | collective-permute-done | bytes 524320 | tf_op jit(solution)/shard_map/ppermute | solution.py:249
  81.2 2.5 %collective-permute-done.3.refs_3_ = bf16[64,4096]{1,0:T(8,128)(2,1)} collective-permute-done((bf16[64,4096]{1,0:T(8,128)(2,1)S(1)}, bf16[64,4096]{1,0:T(8,128)(2,1)}, u32[]{:S(2)}, u32[]{:S(2)}) %collective-permute-start.3) | collective-permute-done | bytes 524320 | tf_op jit(solution)/shard_map/ppermute | solution.py:249
  83.8 0.0 collective-permute-done.5.refs_5_
  83.8 10.4 %collective-permute-done.6.refs_6_ = bf16[64,4096]{1,0:T(8,128)(2,1)} collective-permute-done((bf16[64,4096]{1,0:T(8,128)(2,1)S(1)}, bf16[64,4096]{1,0:T(8,128)(2,1)}, u32[]{:S(2)}, u32[]{:S(2)}) %collective-permute-start.6) | collective-permute-done | bytes 524320 | tf_op jit(solution)/shard_map/ppermute | solution.py:249
  94.2 4.1 %gram.1 = f32[1280,128]{1,0:T(8,128)S(1)} custom-call(s32[8]{0:T(128)S(1)} %stack.44.place_ref, bf16[64,4096]{1,0:T(8,128)(2,1)} %collective-permute-done.refs_0_, bf16[64,4096]{1,0:T(8,128)(2,1)} %collective-permute-done.1.refs_1_, bf16[64,4096]{1,0:T(8,128)(2,1)} %collective-permute-done.2.refs_2_, bf16[64,4096]{1,0:T(8,128)(2,1)} %collective-permute-done.3.refs_3_, ...), custom_call_target="tpu_custom_call" | custom-call | flops 2147483648 | bytes 4849664 | tf_op jit(solution)/shard_map/gram/pallas_call | solution.py:86
  98.3 12.8 %all_to_all.20 = f32[4,320,128]{2,1,0:T(8,128)S(1)} all-to-all(f32[4,320,128]{2,1,0:T(8,128)S(1)} %bitcast.17), channel_id=1, replica_groups=mesh['grp'=4,'dev'=8] {'grp'}, dimensions={0} | all-to-all | bytes 1310720 | tf_op jit(solution)/shard_map/all_to_all | solution.py:106
  111.2 19.6 %all_to_all.21 = f32[8,40,128]{2,1,0:T(8,128)S(1)} all-to-all(f32[8,40,128]{2,1,0:T(8,128)S(1)} %bitcast.26), channel_id=1, replica_groups=mesh['grp'=4,'dev'=8] {'dev'}, dimensions={0} | all-to-all | bytes 327680 | tf_op jit(solution)/shard_map/all_to_all | solution.py:106
  130.8 10.0 %all_to_all.22 = f32[8,40,128]{2,1,0:T(8,128)S(1)} all-to-all(f32[8,40,128]{2,1,0:T(8,128)S(1)} %broadcast_in_dim.6), channel_id=1, replica_groups=mesh['grp'=4,'dev'=8] {'dev'}, dimensions={0} | all-to-all | bytes 327680 | tf_op jit(solution)/shard_map/all_to_all | solution.py:112
  140.8 0.9 broadcast_in_dim.15
  141.6 3.7 %all-to-all-start.3 = ((f32[4,320,128]{2,1,0:T(8,128)}), f32[4,320,128]{2,1,0:T(8,128)S(1)}, u32[]{:S(2)}, u32[]{:S(2)}) async-start(f32[4,320,128]{2,1,0:T(8,128)} %broadcast_in_dim.15), calls=%async_computation.3 | async-start | bytes 1310720 | tf_op jit(solution)/shard_map/all_to_all | solution.py:112
  145.3 0.1 pad_add_fusion.place_ref
  145.4 9.9 %all-to-all-done.3 = f32[4,320,128]{2,1,0:T(8,128)S(1)} async-done(((f32[4,320,128]{2,1,0:T(8,128)}), f32[4,320,128]{2,1,0:T(8,128)S(1)}, u32[]{:S(2)}, u32[]{:S(2)}) %all-to-all-start.3) | async-done | bytes 655392 | tf_op jit(solution)/shard_map/all_to_all | solution.py:112
  155.3 18.3 %triangle.1 = f32[64,128]{1,0:T(8,128)} custom-call(s32[2]{0:T(128)S(1)} %pad_add_fusion.place_ref, f32[1280,128]{1,0:T(8,128)S(1)} %bitcast.16), custom_call_target="tpu_custom_call" | custom-call | flops 134217728 | bytes 1048576 | tf_op jit(solution)/shard_map/triangle/pallas_call | solution.py:211
  (5 shorter events, 0.1 us)
Async XLA Ops:
  6.6 39.7 %collective-permute-start = (bf16[64,4096]{1,0:T(8,128)(2,1)}, bf16[64,4096]{1,0:T(8,128)(2,1)}, u32[]{:S(2)}, u32[]{:S(2)}) collective-permute-start(bf16[64,4096]{1,0:T(8,128)(2,1)} %project.8), channel_id=1, source_target_pairs={{0,4},{1,5},{2,6},{3,7},{4,0},{5,1},{6,2},{7,3},{8,12},{9,13},{10,... | collective-permute-start | bytes 1572872 | tf_op jit(solution)/shard_map/ppermute | solution.py:249
  15.5 35.9 %collective-permute-start.1 = (bf16[64,4096]{1,0:T(8,128)(2,1)S(1)}, bf16[64,4096]{1,0:T(8,128)(2,1)}, u32[]{:S(2)}, u32[]{:S(2)}) collective-permute-start(bf16[64,4096]{1,0:T(8,128)(2,1)S(1)} %project.9), channel_id=1, source_target_pairs={{0,1},{1,0},{2,3},{3,2},{4,5},{5,4},{6,7},{7,6},{8,9},{9,8},{10,11... | collective-permute-start | bytes 1572872 | tf_op jit(solution)/shard_map/ppermute | solution.py:249
  21.9 59.3 %collective-permute-start.2 = (bf16[64,4096]{1,0:T(8,128)(2,1)S(1)}, bf16[64,4096]{1,0:T(8,128)(2,1)}, u32[]{:S(2)}, u32[]{:S(2)}) collective-permute-start(bf16[64,4096]{1,0:T(8,128)(2,1)S(1)} %project.10), channel_id=1, source_target_pairs={{0,5},{1,4},{2,7},{3,6},{4,1},{5,0},{6,3},{7,2},{8,13},{9,12},{10,... | collective-permute-start | bytes 1572872 | tf_op jit(solution)/shard_map/ppermute | solution.py:249
  26.8 57.0 %collective-permute-start.3 = (bf16[64,4096]{1,0:T(8,128)(2,1)S(1)}, bf16[64,4096]{1,0:T(8,128)(2,1)}, u32[]{:S(2)}, u32[]{:S(2)}) collective-permute-start(bf16[64,4096]{1,0:T(8,128)(2,1)S(1)} %project.11), channel_id=1, source_target_pairs={{0,2},{1,3},{2,0},{3,1},{4,6},{5,7},{6,4},{7,5},{8,10},{9,11},{10,... | collective-permute-start | bytes 1572872 | tf_op jit(solution)/shard_map/ppermute | solution.py:249
  33.5 50.3 %collective-permute-start.4 = (bf16[64,4096]{1,0:T(8,128)(2,1)S(1)}, bf16[64,4096]{1,0:T(8,128)(2,1)}, u32[]{:S(2)}, u32[]{:S(2)}) collective-permute-start(bf16[64,4096]{1,0:T(8,128)(2,1)S(1)} %project.12), channel_id=1, source_target_pairs={{0,6},{1,7},{2,4},{3,5},{4,2},{5,3},{6,0},{7,1},{8,14},{9,15},{10,... | collective-permute-start | bytes 1572872 | tf_op jit(solution)/shard_map/ppermute | solution.py:249
  46.3 37.5 %collective-permute-start.5 = (bf16[64,4096]{1,0:T(8,128)(2,1)S(1)}, bf16[64,4096]{1,0:T(8,128)(2,1)}, u32[]{:S(2)}, u32[]{:S(2)}) collective-permute-start(bf16[64,4096]{1,0:T(8,128)(2,1)S(1)} %project.13), channel_id=1, source_target_pairs={{0,7},{1,6},{2,5},{3,4},{4,3},{5,2},{6,1},{7,0},{8,15},{9,14},{10,... | collective-permute-start | bytes 1572872 | tf_op jit(solution)/shard_map/ppermute | solution.py:249
  51.4 42.9 %collective-permute-start.6 = (bf16[64,4096]{1,0:T(8,128)(2,1)S(1)}, bf16[64,4096]{1,0:T(8,128)(2,1)}, u32[]{:S(2)}, u32[]{:S(2)}) collective-permute-start(bf16[64,4096]{1,0:T(8,128)(2,1)S(1)} %project.14), channel_id=1, source_target_pairs={{0,3},{1,2},{2,1},{3,0},{4,7},{5,6},{6,5},{7,4},{8,11},{9,10},{10,... | collective-permute-start | bytes 1572872 | tf_op jit(solution)/shard_map/ppermute | solution.py:249
  141.6 13.7 %all-to-all-start.3 = ((f32[4,320,128]{2,1,0:T(8,128)}), f32[4,320,128]{2,1,0:T(8,128)S(1)}, u32[]{:S(2)}, u32[]{:S(2)}) async-start(f32[4,320,128]{2,1,0:T(8,128)} %broadcast_in_dim.15), calls=%async_computation.3 | async-start | bytes 1310720 | tf_op jit(solution)/shard_map/all_to_all | solution.py:112

commit v3 on v2

v3 whole, which is shorter than its diff:
```python
import functools

import jax
import jax.numpy as jnp
from jax import lax
from jax.experimental import pallas as pl
from jax.experimental.pallas import tpu as pltpu
from jax.sharding import PartitionSpec as P

LANES = 128


def project_kernel(rank, slabs, *refs):
    slab_refs = refs[slabs:2 * slabs]
    factor_ref = refs[2 * slabs]
    out_refs = refs[2 * slabs + 1:-1]
    wide_ref = refs[-1]
    cols, width, depth = slab_refs[0].shape
    half = width // 2
    pitch = width + 1
    lane = lax.broadcasted_iota(jnp.int32, (cols, LANES), 1)
    for i, slab_ref in enumerate(slab_refs):
        flat = slab_ref[...].reshape(cols * width, depth)
        wide = jnp.dot(flat, factor_ref[...], preferred_element_type=jnp.float32)
        base = i * cols * pitch
        for c in range(cols):
            wide_ref[base + c * pitch:base + c * pitch + width, :] = wide[c * width:(c + 1) * width, :]
        for s in range(half):
            low = wide_ref[pl.ds(base + s, cols, stride=pitch), :]
            high = wide_ref[pl.ds(base + s + half, cols, stride=pitch), :]
            both = jnp.where(lane < rank, low, high).astype(jnp.bfloat16)
            at = (i * half + s) * LANES
            out_refs[0][:, at:at + LANES] = both
            if i:
                out_refs[i][:, s * LANES:(s + 1) * LANES] = both


def project(slab, factor_pair, rank, dests, width):
    cols, total_width, depth = slab.shape
    block_cols = 16
    out_width = width * rank
    slabs = len(dests)
    widths = [slabs * out_width] + [out_width] * (slabs - 1)
    grid_spec = pltpu.PrefetchScalarGridSpec(
        num_scalar_prefetch=slabs,
        grid=(cols // block_cols,),
        in_specs=[
            pl.BlockSpec((block_cols, width, depth), lambda c, *d, i=i: (c, d[i][0], 0))
            for i in range(slabs)
        ]
        + [pl.BlockSpec(factor_pair.shape, lambda c, *d: (0, 0))],
        out_specs=[pl.BlockSpec((block_cols, w), lambda c, *d: (c, 0)) for w in widths],
        scratch_shapes=[pltpu.VMEM((slabs * block_cols * (width + 1) + 7, LANES), jnp.float32)],
    )
    return pl.pallas_call(
        functools.partial(project_kernel, rank, slabs),
        out_shape=[jax.ShapeDtypeStruct((cols, w), jnp.bfloat16) for w in widths],
        grid_spec=grid_spec,
        compiler_params=pltpu.CompilerParams(vmem_limit_bytes=44 * 2**20),
        cost_estimate=pl.CostEstimate(
            flops=8 * slabs * cols * width * depth * rank,
            bytes_accessed=2 * slabs * cols * width * depth + 2 * cols * sum(widths),
            transcendentals=0,
        ),
        name="project",
    )(*[d.reshape(1) for d in dests], *[slab] * slabs, factor_pair)


def upper_blocks(count):
    return [(a, b) for a in range(count) for b in range(a, count)]


def gram_near_kernel(scale, width, count, place_ref, *refs):
    pieces = refs[:count]
    out_ref, full_ref = refs[count:]
    cols = pieces[0].shape[0]
    for i, piece in enumerate(pieces):
        start = pl.multiple_of(place_ref[i] * cols, 16)
        first = 0 if i != 1 else width
        full_ref[pl.ds(start, cols), first:first + piece.shape[1]] = piece[...]
    order = full_ref.shape[0]
    product = lax.dot_general(
        full_ref[...], full_ref[...], (((1,), (1,)), ((), ())), preferred_element_type=jnp.float32
    ) * scale
    for n, (a, b) in enumerate(upper_blocks(order // LANES)):
        out_ref[n * LANES:(n + 1) * LANES, :] = product[a * LANES:(a + 1) * LANES, b * LANES:(b + 1) * LANES]


def gram_cross_kernel(scale, width, count, place_ref, *refs):
    pieces = refs[:count]
    out_ref, full_ref = refs[count:]
    cols = pieces[0].shape[0]
    for i, piece in enumerate(pieces):
        start = pl.multiple_of(place_ref[i] * cols, 16)
        full_ref[pl.ds(start, cols), :] = piece[:, :width]
    half = full_ref.shape[0] // 2
    product = lax.dot_general(
        full_ref[:half, :], full_ref[half:, :], (((1,), (1,)), ((), ())), preferred_element_type=jnp.float32
    ) * scale
    blocks = half // LANES
    for a in range(blocks):
        for b in range(blocks):
            n = a * blocks + b
            out_ref[n * LANES:(n + 1) * LANES, :] = product[a * LANES:(a + 1) * LANES, b * LANES:(b + 1) * LANES]


def gram(kernel, pieces, places, scale, width, scratch, blocks, name):
    rows = blocks * LANES
    return pl.pallas_call(
        functools.partial(kernel, scale, width, len(pieces)),
        out_shape=jax.ShapeDtypeStruct((rows, LANES), jnp.float32),
        in_specs=[pl.BlockSpec(memory_space=pltpu.SMEM)]
        + [pl.BlockSpec(memory_space=pltpu.VMEM)] * len(pieces),
        out_specs=pl.BlockSpec(memory_space=pltpu.VMEM),
        scratch_shapes=[pltpu.VMEM(scratch, jnp.bfloat16)],
        compiler_params=pltpu.CompilerParams(vmem_limit_bytes=40 * 2**20),
        cost_estimate=pl.CostEstimate(
            flops=2 * scratch[0] * scratch[0] * scratch[1],
            bytes_accessed=2 * scratch[0] * scratch[1] + 4 * rows * LANES,
            transcendentals=0,
        ),
        name=name,
    )(places, *pieces)


BOTH = ("grp", "dev")


def exchange(x):
    return lax.all_to_all(x, BOTH, split_axis=0, concat_axis=0, tiled=True)


def shares(x, devices):
    rows = x.shape[0]
    x = jnp.pad(x, ((0, -rows % (8 * devices)), (0, 0)))
    return x.reshape(devices, x.shape[0] // devices, LANES)


def gather(x, devices):
    return exchange(jnp.broadcast_to(x[None], (devices, *x.shape)))


def spread_lane(rows, lane):
    return jnp.broadcast_to(rows[:, lane:lane + 1], rows.shape)


def spread_row(rows, row):
    return jnp.broadcast_to(rows[row:row + 1, :], rows.shape)


def factor_block(block, step):
    lane = lax.broadcasted_iota(jnp.int32, (step, LANES), 1)
    row = lax.broadcasted_iota(jnp.int32, (step, LANES), 0)
    rows = [block[i * step:(i + 1) * step, :] for i in range(LANES // step)]
    tri_rows, inv_rows = [], []
    for t, head in enumerate(rows):
        first = t * step
        inside = (lane >= first) & (lane < first + step)
        spread = [spread_lane(head, first + b) for b in range(step)]
        s = {(a, b): spread_row(spread[b], a) for a in range(step) for b in range(a, step)}
        r, inv_diag = {}, []
        for k in range(step):
            inv = lax.rsqrt(s[k, k])
            inv_diag.append(inv)
            for b in range(k, step):
                r[k, b] = s[k, b] * inv
            for a in range(k + 1, step):
                for b in range(a, step):
                    s[a, b] = s[a, b] - r[k, a] * r[k, b]
        tri, mix = [], []
        for k in range(step):
            raw = spread_row(head, k)
            x = raw
            y = jnp.where(inside, jnp.where(lane == first + k, 1.0, 0.0), raw)
            for m in range(k):
                x = x - r[m, k] * tri[m]
                y = y - r[m, k] * mix[m]
            tri.append(x * inv_diag[k])
            mix.append(y * inv_diag[k])
        tri_out, mix_out = tri[0], mix[0]
        for k in range(1, step):
            tri_out = jnp.where(row == k, tri[k], tri_out)
            mix_out = jnp.where(row == k, mix[k], mix_out)
        tri_rows.append(jnp.where(lane >= row + first, tri_out, 0.0))
        inv_rows.append(jnp.where(lane <= row + first, mix_out, 0.0))
        for i in range(t + 1, LANES // step):
            col, held = [], jnp.where(inside, 0.0, rows[i])
            for k in range(step):
                c = spread_lane(rows[i], first + k)
                for m in range(k):
                    c = c - r[m, k] * col[m]
                col.append(c * inv_diag[k])
                held = held - col[k] * mix[k]
            rows[i] = held
    return tri_rows, inv_rows


HIGH = lax.Precision.HIGHEST


def block_at(ref, a, b):
    return ref.at[a * LANES:(a + 1) * LANES, b * LANES:(b + 1) * LANES]


def factor_into(tri_ref, inv_ref, work_ref, p):
    step = 8
    tri_rows, inv_rows = factor_block(block_at(work_ref, p, p)[...], step)
    for i in range(LANES // step):
        at = slice(p * LANES + i * step, p * LANES + (i + 1) * step)
        tri_ref[at, p * LANES:(p + 1) * LANES] = tri_rows[i]
        inv_ref[at, :] = inv_rows[i]


def solve_row(tri_ref, inv_ref, work_ref, p, q):
    block_at(tri_ref, p, q)[...] = jnp.dot(
        inv_ref[p * LANES:(p + 1) * LANES, :], block_at(work_ref, p, q)[...],
        precision=HIGH, preferred_element_type=jnp.float32,
    )


def take_off(tri_ref, work_ref, p, a, b):
    block_at(work_ref, a, b)[...] -= lax.dot_general(
        block_at(tri_ref, p, a)[...], block_at(tri_ref, p, b)[...],
        (((0,), (0,)), ((), ())), precision=HIGH, preferred_element_type=jnp.float32,
    )


def first_triangle_kernel(count, blocks_ref, tri_ref, inv_ref, work_ref):
    for n, (a, b) in enumerate(upper_blocks(count)):
        block_at(work_ref, a, b)[...] = blocks_ref[n * LANES:(n + 1) * LANES, :]
    tri_ref[...] = jnp.zeros_like(tri_ref)
    for p in range(count):
        factor_into(tri_ref, inv_ref, work_ref, p)
        for q in range(p + 1, count):
            solve_row(tri_ref, inv_ref, work_ref, p, q)
        for a, b in upper_blocks(count):
            if a > p:
                take_off(tri_ref, work_ref, p, a, b)


def first_triangle(blocks, count):
    size = count * LANES
    return pl.pallas_call(
        functools.partial(first_triangle_kernel, count),
        out_shape=[
            jax.ShapeDtypeStruct((size, size), jnp.float32),
            jax.ShapeDtypeStruct((size, LANES), jnp.float32),
        ],
        in_specs=[pl.BlockSpec(memory_space=pltpu.VMEM)],
        out_specs=[pl.BlockSpec(memory_space=pltpu.VMEM)] * 2,
        scratch_shapes=[pltpu.VMEM((size, size), jnp.float32)],
        compiler_params=pltpu.CompilerParams(vmem_limit_bytes=32 * 2**20),
        cost_estimate=pl.CostEstimate(
            flops=size**3, bytes_accessed=8 * size * size, transcendentals=size
        ),
        name="first_triangle",
    )(blocks)


def last_triangle_kernel(count, place_ref, done_ref, done_inv_ref, cross_ref, last_ref, out_ref, work_ref, tri_ref, inv_ref):
    half = count // 2
    size = half * LANES
    for a in range(half):
        for b in range(half):
            n = a * half + b
            block_at(work_ref, a, half + b)[...] = cross_ref[n * LANES:(n + 1) * LANES, :]
    for n, (a, b) in enumerate(upper_blocks(half)):
        block_at(work_ref, half + a, half + b)[...] = last_ref[n * LANES:(n + 1) * LANES, :]
    tri_ref[...] = jnp.zeros_like(tri_ref)
    tri_ref[:size, :size] = done_ref[...]
    inv_ref[:size, :] = done_inv_ref[...]
    for p in range(count):
        if p >= half:
            factor_into(tri_ref, inv_ref, work_ref, p)
        for q in range(max(p + 1, half), count):
            solve_row(tri_ref, inv_ref, work_ref, p, q)
        for a, b in upper_blocks(count):
            if a > p and b >= half:
                take_off(tri_ref, work_ref, p, a, b)
    out_rows = out_ref.shape[0]
    row = pl.multiple_of(place_ref[0] * out_rows, 8)
    col = pl.multiple_of(place_ref[1] * LANES, LANES)
    out_ref[...] = tri_ref[pl.ds(row, out_rows), pl.ds(col, LANES)]


def last_triangle(done, done_inv, cross, last, order):
    row_count = order // lax.axis_size("dev")
    col_count = order // lax.axis_size("grp")
    grp = lax.axis_index("grp")
    place = jnp.stack([lax.axis_index("dev"), grp * col_count // LANES]).astype(jnp.int32)
    out = pl.pallas_call(
        functools.partial(last_triangle_kernel, order // LANES),
        out_shape=jax.ShapeDtypeStruct((row_count, LANES), jnp.float32),
        in_specs=[pl.BlockSpec(memory_space=pltpu.SMEM)] + [pl.BlockSpec(memory_space=pltpu.VMEM)] * 4,
        out_specs=pl.BlockSpec(memory_space=pltpu.VMEM),
        scratch_shapes=[
            pltpu.VMEM((order, order), jnp.float32),
            pltpu.VMEM((order, order), jnp.float32),
            pltpu.VMEM((order, LANES), jnp.float32),
        ],
        compiler_params=pltpu.CompilerParams(vmem_limit_bytes=32 * 2**20),
        cost_estimate=pl.CostEstimate(
            flops=order**3, bytes_accessed=4 * order * order, transcendentals=order
        ),
        name="last_triangle",
    )(place, done, done_inv, cross, last)
    if col_count == LANES:
        return out
    return lax.dynamic_slice(out, (0, grp * col_count % LANES), (row_count, col_count))


def per_device(tensor_slab, mode_factor):
    depth, cols, slab_depth, species = tensor_slab.shape
    rank = mode_factor.shape[1]
    n_dev = lax.axis_size("dev")
    n_grp = lax.axis_size("grp")
    devices = n_dev * n_grp
    me = lax.axis_index("dev").astype(jnp.int32)
    slab = tensor_slab.transpose(1, 2, 3, 0).reshape(cols, slab_depth * species, depth)
    width = slab_depth * species // n_dev
    out_width = width * rank
    factor_pair = jnp.concatenate([mode_factor, mode_factor], axis=1)
    scale = 1.0 / (rank * slab_depth * species * n_grp)
    half = n_dev // 2
    order = cols * n_dev

    def partner(offset):
        return jnp.bitwise_xor(me, offset)

    def send(piece, offset):
        return lax.ppermute(piece, "dev", [(i, i ^ offset) for i in range(n_dev)])

    [mirror] = project(slab, factor_pair, rank, [partner(half)], width)
    far = [send(mirror, half)]
    near = []
    for offset in range(1, half):
        dests = [partner(offset), partner(offset + half)]
        if offset == 1:
            mirror, *dests = lax.optimization_barrier((mirror, *dests))
        elif offset == half - 1:
            far[0], *dests = lax.optimization_barrier((far[0], *dests))
        both, other = project(slab, factor_pair, rank, dests, width)
        near.append(send(both, offset))
        far.append(send(other, offset + half))
    [own] = project(slab, factor_pair, rank, [me], width)

    near_places = jnp.stack([me % half, me % half] + [partner(o) % half for o in range(1, half)])
    part = gram(
        gram_near_kernel, [own, mirror, *near], near_places, scale, out_width,
        (order // 2, 2 * out_width), len(upper_blocks(order // 2 // LANES)), "gram_near",
    )
    parts = exchange(shares(part, devices))
    parts = parts.reshape(n_grp, 2, half, *parts.shape[1:]).sum(axis=(0, 2))
    halves = gather(parts, devices)
    halves = halves.transpose(1, 0, 2, 3).reshape(2, -1, LANES)
    done, done_inv = first_triangle(halves[0], order // 2 // LANES)

    places = jnp.stack([partner(o) for o in [*range(half, n_dev), 0, *range(1, half)]])
    own, done = lax.optimization_barrier((own, done))
    cross = gram(
        gram_cross_kernel, [*far, own, *near], places, scale, out_width,
        (order, out_width), (order // 2 // LANES) ** 2, "gram_cross",
    )
    cross = exchange(shares(cross, devices)).sum(axis=0)
    cross = gather(cross, devices).reshape(-1, LANES)
    return last_triangle(done, done_inv, cross, halves[1], order)


def solution(mesh):
    in_specs = (P(None, "dev", "grp", None), P())
    out_specs = P("dev", "grp")
    return jax.shard_map(
        per_device, mesh=mesh, in_specs=in_specs, out_specs=out_specs, check_vma=False
    )
```

time: 175 us -> 225 us (1.29)
  waiting for transfers between devices: 48.4 us -> 92.7 us
  Pallas kernels: 61.7 us -> 52 us
  blocking collectives: 42.4 us -> 49.7 us
  local copies, waits for them, and re-layouts: 1.93 us -> 8.07 us
  starting transfers between devices: 18.8 us -> 21.7 us
    all_to_all x1 -> x2, waiting for transfers between devices: 9.94 us -> 53 us  [exchange(): return lax.all_to_all(x, BOTH, split_axis=0, concat_axis=0, tiled=True)]
    pallas_call x10 -> x9, Pallas kernels: 61.7 us -> 52 us  [the longest x5 27.2 us: project(): pl.pallas_call(functools.partial(project_kernel, rank, slabs), out_shape=...]
    all_to_all x3 -> x2, blocking collectives: 42.4 us -> 49.7 us  [exchange(): return lax.all_to_all(x, BOTH, split_axis=0, concat_axis=0, tiled=True)]
    unnamed x1 -> x13, local copies, waits for them, and re-layouts: 0.95 us -> 5.23 us
    all_to_all x1 -> x2, starting transfers between devices: 3.66 us -> 5.59 us  [exchange(): return lax.all_to_all(x, BOTH, split_axis=0, concat_axis=0, tiled=True)]
  transfers between devices with their start and end apart: 8 -> 9, of which waited for: 5 -> 6; matrix products, arithmetic and copies ran while one was open for 0% -> 1% of each run, Pallas kernels for 19% -> 14%
where the time goes in v3:
time: 225 us
  waiting for transfers between devices  92.7 us (41%)
  Pallas kernels  52 us (23%)
  blocking collectives  49.7 us (22%)
  starting transfers between devices  21.7 us (10%)
  local copies, waits for them, and re-layouts  8.07 us (4%)
    all_to_all x2, waiting for transfers between devices, exchange(): return lax.all_to_all(x, BOTH, split_axis=0, concat_axis=0, tiled=True)  53 us
    all_to_all x2, blocking collectives, exchange(): return lax.all_to_all(x, BOTH, split_axis=0, concat_axis=0, tiled=True)  49.7 us
    ppermute x7, waiting for transfers between devices, send(): return lax.ppermute(piece, 'dev', [(i, i ^ offset) for i in range(n_dev)])  39.7 us
    pallas_call x5, Pallas kernels, project(): pl.pallas_call(functools.partial(project_kernel, rank, slabs), out_shape=...  27.2 us
    ppermute x7, starting transfers between devices, send(): return lax.ppermute(piece, 'dev', [(i, i ^ offset) for i in range(n_dev)])  16.1 us
    pallas_call x1, Pallas kernels, last_triangle(): pl.pallas_call(functools.partial(last_triangle_kernel, order // LANES), o...  10.9 us
    pallas_call x1, Pallas kernels, first_triangle(): pl.pallas_call(functools.partial(first_triangle_kernel, count), out_shape...  8.4 us
    all_to_all x2, starting transfers between devices, exchange(): return lax.all_to_all(x, BOTH, split_axis=0, concat_axis=0, tiled=True)  5.59 us
  transfers between devices with their start and end apart: 9, of which 6 were waited for; matrix products, arithmetic and copies ran while one was open for 1% of the time, Pallas kernels for 14%

profile of v3, /device:TPU:0, one launch (start us, length us, event | category | flops | bytes accessed | tf_op | source)
XLA Modules:
  0.0 224.6 jit_solution(6786271032808131780)
XLA Ops:
  0.0 1.0 copy.5
  1.1 4.0 %project.6.refs_1_ = bf16[64,4096]{1,0:T(8,128)(2,1)S(1)} custom-call(s32[1]{0:T(128)} %bitcast.8.refs_0_, bf16[64,512,512]{2,1,0:T(8,128)(2,1)} %bitcast.31, bf16[512,128]{1,0:T(8,128)(2,1)S(1)} %pad_maximum_fusion.refs_2_.refs_4_), custom_call_target="tpu_custom_call" | custom-call | flops 1073741824 | bytes 4718592 | tf_op jit(solution)/shard_map/project/pallas_call | solution.py:55
  5.1 4.1 %collective-permute-start.2 = (bf16[64,4096]{1,0:T(8,128)(2,1)S(1)}, bf16[64,4096]{1,0:T(8,128)(2,1)S(1)}, u32[]{:S(2)}, u32[]{:S(2)}) collective-permute-start(bf16[64,4096]{1,0:T(8,128)(2,1)S(1)} %project.6.refs_1_), channel_id=1, source_target_pairs={{0,4},{1,5},{2,6},{3,7},{4,0},{5,1},{6,2},{7,3},{8,12},{9,13},{10,... | collective-permute-start | bytes 1572872 | tf_op jit(solution)/shard_map/ppermute | solution.py:331
  9.2 6.4 %project.7 = (bf16[64,8192]{1,0:T(8,128)(2,1)}, bf16[64,4096]{1,0:T(8,128)(2,1)S(1)}) custom-call(s32[1]{0:T(128)} %bitcast.10.refs_0_, s32[1]{0:T(128)} %bitcast.11.refs_1_, bf16[64,512,512]{2,1,0:T(8,128)(2,1)} %bitcast.32, bf16[64,512,512]{2,1,0:T(8,128)(2,1)} %bitcast.33, bf16[512,128]{1,0:T(8,128)(2,1)S(1)} %pad_maximum_fusion.refs_2_.refs_4_), custom_call_target="tpu_custom_call" | custom-call | flops 2147483648 | bytes 9961472 | tf_op jit(solution)/shard_map/project/pallas_call | solution.py:55
  16.4 1.5 collective-permute-start
  17.9 6.4 %project.8 = (bf16[64,8192]{1,0:T(8,128)(2,1)}, bf16[64,4096]{1,0:T(8,128)(2,1)S(1)}) custom-call(s32[1]{0:T(128)} %bitcast.12.refs_0_, s32[1]{0:T(128)} %bitcast.13.refs_1_, bf16[64,512,512]{2,1,0:T(8,128)(2,1)} %bitcast.34, bf16[64,512,512]{2,1,0:T(8,128)(2,1)} %bitcast.35, bf16[512,128]{1,0:T(8,128)(2,1)S(1)} %pad_maximum_fusion.refs_2_.refs_4_), custom_call_target="tpu_custom_call" | custom-call | flops 2147483648 | bytes 9961472 | tf_op jit(solution)/shard_map/project/pallas_call | solution.py:55
  25.1 1.6 collective-permute-start.1
  26.6 5.8 %collective-permute-done.2.refs_0_ = bf16[64,4096]{1,0:T(8,128)(2,1)S(1)} collective-permute-done((bf16[64,4096]{1,0:T(8,128)(2,1)S(1)}, bf16[64,4096]{1,0:T(8,128)(2,1)S(1)}, u32[]{:S(2)}, u32[]{:S(2)}) %collective-permute-start.2) | collective-permute-done | bytes 524320 | tf_op jit(solution)/shard_map/ppermute | solution.py:331
  32.4 6.5 %project.9 = (bf16[64,8192]{1,0:T(8,128)(2,1)}, bf16[64,4096]{1,0:T(8,128)(2,1)S(1)}) custom-call(s32[1]{0:T(128)} %bitcast.14.refs_0_, s32[1]{0:T(128)} %bitcast.15.refs_1_, bf16[64,512,512]{2,1,0:T(8,128)(2,1)} %bitcast.36, bf16[64,512,512]{2,1,0:T(8,128)(2,1)} %bitcast.37, bf16[512,128]{1,0:T(8,128)(2,1)S(1)} %pad_maximum_fusion.refs_2_.refs_4_), custom_call_target="tpu_custom_call" | custom-call | flops 2147483648 | bytes 9961472 | tf_op jit(solution)/shard_map/project/pallas_call | solution.py:55
  39.0 0.8 copy-done.4
  39.8 1.6 collective-permute-start.3
  41.5 4.0 %project.5.refs_0_.refs_4_ = bf16[64,4096]{1,0:T(8,128)(2,1)S(1)} custom-call(s32[1]{0:T(128)} %bitcast.refs_0_, bf16[64,512,512]{2,1,0:T(8,128)(2,1)} %bitcast.38, bf16[512,128]{1,0:T(8,128)(2,1)S(1)} %pad_maximum_fusion.refs_2_.refs_4_), custom_call_target="tpu_custom_call" | custom-call | flops 1073741824 | bytes 4718592 | tf_op jit(solution)/shard_map/project/pallas_call | solution.py:55
  45.5 9.4 %collective-permute-done.1.refs_3_.refs_6_ = bf16[64,8192]{1,0:T(8,128)(2,1)S(1)} collective-permute-done((bf16[64,8192]{1,0:T(8,128)(2,1)}, bf16[64,8192]{1,0:T(8,128)(2,1)S(1)}, u32[]{:S(2)}, u32[]{:S(2)}) %collective-permute-start.1) | collective-permute-done | bytes 1048608 | tf_op jit(solution)/shard_map/ppermute | solution.py:331
  54.9 23.5 %collective-permute-done.3.refs_4_.refs_7_ = bf16[64,8192]{1,0:T(8,128)(2,1)} collective-permute-done((bf16[64,8192]{1,0:T(8,128)(2,1)}, bf16[64,8192]{1,0:T(8,128)(2,1)}, u32[]{:S(2)}, u32[]{:S(2)}) %collective-permute-start.3) | collective-permute-done | bytes 1048608 | tf_op jit(solution)/shard_map/ppermute | solution.py:331
  78.4 2.8 %gram_near.1 = f32[384,128]{1,0:T(8,128)S(1)} custom-call(s32[5]{0:T(128)S(1)} %stack.51.place_ref, bf16[64,4096]{1,0:T(8,128)(2,1)S(1)} %project.5.refs_0_.refs_4_, bf16[64,4096]{1,0:T(8,128)(2,1)S(1)} %project.6.refs_1_, bf16[64,8192]{1,0:T(8,128)(2,1)S(1)} %collective-permute-done.refs_2_.refs_5_, ...), custom_call_target="tpu_custom_call" | custom-call | flops 1073741824 | bytes 4390912 | tf_op jit(solution)/shard_map/gram_near/pallas_call | solution.py:109
  81.2 15.2 %all_to_all.20 = f32[32,16,128]{2,1,0:T(8,128)S(1)} all-to-all(f32[32,16,128]{2,1,0:T(8,128)S(1)} %bitcast.40), channel_id=1, replica_groups=mesh['grp'=4,'dev'=8] {'grp','dev'}, dimensions={0} | all-to-all | bytes 524288 | tf_op jit(solution)/shard_map/all_to_all | solution.py:130
  96.5 0.9 broadcast_in_dim.4
  97.3 2.8 %all-to-all-start.1 = ((f32[32,2,16,128]{3,2,1,0:T(8,128)}), f32[32,2,16,128]{3,2,1,0:T(8,128)S(1)}, u32[]{:S(2)}, u32[]{:S(2)}) async-start(f32[32,2,16,128]{3,2,1,0:T(8,128)} %broadcast_in_dim.4), calls=%async_computation.1 | async-start | bytes 1048576 | tf_op jit(solution)/shard_map/all_to_all | solution.py:130
  100.1 3.5 %collective-permute-start.4 = (bf16[64,4096]{1,0:T(8,128)(2,1)}, bf16[64,4096]{1,0:T(8,128)(2,1)}, u32[]{:S(2)}, u32[]{:S(2)}) collective-permute-start(bf16[64,4096]{1,0:T(8,128)(2,1)} %copy-done.2), channel_id=1, source_target_pairs={{0,5},{1,4},{2,7},{3,6},{4,1},{5,0},{6,3},{7,2},{8,13},{9,12},{10,... | collective-permute-start | bytes 1572872 | tf_op jit(solution)/shard_map/ppermute | solution.py:331
  103.6 1.4 collective-permute-start.5
  105.0 2.4 %collective-permute-start.6 = (bf16[64,4096]{1,0:T(8,128)(2,1)}, bf16[64,4096]{1,0:T(8,128)(2,1)}, u32[]{:S(2)}, u32[]{:S(2)}) collective-permute-start(bf16[64,4096]{1,0:T(8,128)(2,1)} %copy-done.4), channel_id=1, source_target_pairs={{0,7},{1,6},{2,5},{3,4},{4,3},{5,2},{6,1},{7,0},{8,15},{9,14},{10,... | collective-permute-start | bytes 1572872 | tf_op jit(solution)/shard_map/ppermute | solution.py:331
  107.5 42.7 %all-to-all-done.1 = f32[32,2,16,128]{3,2,1,0:T(8,128)S(1)} async-done(((f32[32,2,16,128]{3,2,1,0:T(8,128)}), f32[32,2,16,128]{3,2,1,0:T(8,128)S(1)}, u32[]{:S(2)}, u32[]{:S(2)}) %all-to-all-start.1) | async-done | bytes 524320 | tf_op jit(solution)/shard_map/all_to_all | solution.py:130
  150.2 0.8 copy-done.5
  151.0 1.1 fusion
  152.0 8.4 %first_triangle.1 = (f32[256,256]{1,0:T(8,128)S(1)}, f32[256,128]{1,0:T(8,128)S(1)}) custom-call(f32[512,128]{1,0:T(8,128)S(1)} %bitcast.29), custom_call_target="tpu_custom_call" | custom-call | flops 16777216 | bytes 524288 | tf_op jit(solution)/shard_map/first_triangle/pallas_call | solution.py:243
  160.4 1.0 collective-permute-done.4.refs_1_
  161.4 1.0 copy-done.1
  162.5 2.7 %gram_cross.1 = f32[512,128]{1,0:T(8,128)S(1)} custom-call(s32[8]{0:T(128)S(1)} %stack.56.place_ref, bf16[64,4096]{1,0:T(8,128)(2,1)S(1)} %copy-done.1, bf16[64,4096]{1,0:T(8,128)(2,1)} %collective-permute-done.4.refs_1_, bf16[64,4096]{1,0:T(8,128)(2,1)} %collective-permute-done.5.refs_2_, bf16[64,4096]{1,0:T(8,128)(2,1)} %collective-permute-done.6.refs_3_, ...), custom_call_target="tpu_custom_call" | custom-call | flops 2147483648 | bytes 4456448 | tf_op jit(solution)/shard_map/gram_cross/pallas_call | solution.py:109
  165.2 34.5 %all_to_all.21 = f32[32,16,128]{2,1,0:T(8,128)S(1)} all-to-all(f32[32,16,128]{2,1,0:T(8,128)S(1)} %bitcast.30), channel_id=1, replica_groups=mesh['grp'=4,'dev'=8] {'grp','dev'}, dimensions={0} | all-to-all | bytes 524288 | tf_op jit(solution)/shard_map/all_to_all | solution.py:130
  200.5 2.8 %all-to-all-start.3 = ((f32[32,16,128]{2,1,0:T(8,128)}), f32[32,16,128]{2,1,0:T(8,128)S(1)}, u32[]{:S(2)}, u32[]{:S(2)}) async-start(f32[32,16,128]{2,1,0:T(8,128)} %broadcast_in_dim.5), calls=%async_computation.3 | async-start | bytes 524288 | tf_op jit(solution)/shard_map/all_to_all | solution.py:130
  203.4 10.3 %all-to-all-done.3 = f32[32,16,128]{2,1,0:T(8,128)S(1)} async-done(((f32[32,16,128]{2,1,0:T(8,128)}), f32[32,16,128]{2,1,0:T(8,128)S(1)}, u32[]{:S(2)}, u32[]{:S(2)}) %all-to-all-start.3) | async-done | bytes 262176 | tf_op jit(solution)/shard_map/all_to_all | solution.py:130
  213.7 10.9 %last_triangle.1 = f32[64,128]{1,0:T(8,128)} custom-call(s32[2]{0:T(128)S(1)} %pad_add_fusion.place_ref, f32[256,256]{1,0:T(8,128)S(1)} %get-tuple-element.30.done_ref, f32[256,128]{1,0:T(8,128)S(1)} %get-tuple-element.31.done_inv_ref, f32[512,128]{1,0:T(8,128)S(1)} %bitcast.27, f32[512,128]{1,0:T(8,128)S(1)} %bitcast.28), custom_call_target="tpu_custom_call" | custom-call | flops 134217728 | bytes 1048576 | tf_op jit(solution)/shard_map/last_triangle/pallas_call | solution.py:291
  (20 shorter events, 2.8 us)
Async XLA Ops:
  5.1 27.4 %collective-permute-start.2 = (bf16[64,4096]{1,0:T(8,128)(2,1)S(1)}, bf16[64,4096]{1,0:T(8,128)(2,1)S(1)}, u32[]{:S(2)}, u32[]{:S(2)}) collective-permute-start(bf16[64,4096]{1,0:T(8,128)(2,1)S(1)} %project.6.refs_1_), channel_id=1, source_target_pairs={{0,4},{1,5},{2,6},{3,7},{4,0},{5,1},{6,2},{7,3},{8,12},{9,13},{10,... | collective-permute-start | bytes 1572872 | tf_op jit(solution)/shard_map/ppermute | solution.py:331
  15.6 0.8 copy-start.2
  16.4 29.1 %collective-permute-start = (bf16[64,8192]{1,0:T(8,128)(2,1)}, bf16[64,8192]{1,0:T(8,128)(2,1)S(1)}, u32[]{:S(2)}, u32[]{:S(2)}) collective-permute-start(bf16[64,8192]{1,0:T(8,128)(2,1)} %get-tuple-element.24), channel_id=1, source_target_pairs={{0,1},{1,0},{2,3},{3,2},{4,5},{5,4},{6,7},{7,6},{8,9},{9,8},{10,11... | collective-permute-start | bytes 3145736 | tf_op jit(solution)/shard_map/ppermute | solution.py:331
  24.3 0.8 copy-start.3
  25.1 29.8 %collective-permute-start.1 = (bf16[64,8192]{1,0:T(8,128)(2,1)}, bf16[64,8192]{1,0:T(8,128)(2,1)S(1)}, u32[]{:S(2)}, u32[]{:S(2)}) collective-permute-start(bf16[64,8192]{1,0:T(8,128)(2,1)} %get-tuple-element.25), channel_id=1, source_target_pairs={{0,2},{1,3},{2,0},{3,1},{4,6},{5,7},{6,4},{7,5},{8,10},{9,11},{10,... | collective-permute-start | bytes 3145736 | tf_op jit(solution)/shard_map/ppermute | solution.py:331
  32.4 6.5 %copy-start = (bf16[64,4096]{1,0:T(8,128)(2,1)}, bf16[64,4096]{1,0:T(8,128)(2,1)S(1)}, u32[]{:S(2)}) copy-start(bf16[64,4096]{1,0:T(8,128)(2,1)S(1)} %collective-permute-done.2.refs_0_) | copy-start | bytes 1572868
  39.0 0.8 copy-start.4
  39.8 38.6 %collective-permute-start.3 = (bf16[64,8192]{1,0:T(8,128)(2,1)}, bf16[64,8192]{1,0:T(8,128)(2,1)}, u32[]{:S(2)}, u32[]{:S(2)}) collective-permute-start(bf16[64,8192]{1,0:T(8,128)(2,1)} %get-tuple-element.28), channel_id=1, source_target_pairs={{0,3},{1,2},{2,1},{3,0},{4,7},{5,6},{6,5},{7,4},{8,11},{9,10},{10,... | collective-permute-start | bytes 3145736 | tf_op jit(solution)/shard_map/ppermute | solution.py:331
  97.3 52.8 %all-to-all-start.1 = ((f32[32,2,16,128]{3,2,1,0:T(8,128)}), f32[32,2,16,128]{3,2,1,0:T(8,128)S(1)}, u32[]{:S(2)}, u32[]{:S(2)}) async-start(f32[32,2,16,128]{3,2,1,0:T(8,128)} %broadcast_in_dim.4), calls=%async_computation.1 | async-start | bytes 1048576 | tf_op jit(solution)/shard_map/all_to_all | solution.py:130
  100.1 61.3 %collective-permute-start.4 = (bf16[64,4096]{1,0:T(8,128)(2,1)}, bf16[64,4096]{1,0:T(8,128)(2,1)}, u32[]{:S(2)}, u32[]{:S(2)}) collective-permute-start(bf16[64,4096]{1,0:T(8,128)(2,1)} %copy-done.2), channel_id=1, source_target_pairs={{0,5},{1,4},{2,7},{3,6},{4,1},{5,0},{6,3},{7,2},{8,13},{9,12},{10,... | collective-permute-start | bytes 1572872 | tf_op jit(solution)/shard_map/ppermute | solution.py:331
  103.6 57.8 %collective-permute-start.5 = (bf16[64,4096]{1,0:T(8,128)(2,1)}, bf16[64,4096]{1,0:T(8,128)(2,1)}, u32[]{:S(2)}, u32[]{:S(2)}) collective-permute-start(bf16[64,4096]{1,0:T(8,128)(2,1)} %copy-done.3), channel_id=1, source_target_pairs={{0,6},{1,7},{2,4},{3,5},{4,2},{5,3},{6,0},{7,1},{8,14},{9,15},{10,... | collective-permute-start | bytes 1572872 | tf_op jit(solution)/shard_map/ppermute | solution.py:331
  105.0 56.4 %collective-permute-start.6 = (bf16[64,4096]{1,0:T(8,128)(2,1)}, bf16[64,4096]{1,0:T(8,128)(2,1)}, u32[]{:S(2)}, u32[]{:S(2)}) collective-permute-start(bf16[64,4096]{1,0:T(8,128)(2,1)} %copy-done.4), channel_id=1, source_target_pairs={{0,7},{1,6},{2,5},{3,4},{4,3},{5,2},{6,1},{7,0},{8,15},{9,14},{10,... | collective-permute-start | bytes 1572872 | tf_op jit(solution)/shard_map/ppermute | solution.py:331
  150.2 0.8 copy-start.5
  161.4 1.0 copy-start.1
  200.5 13.2 %all-to-all-start.3 = ((f32[32,16,128]{2,1,0:T(8,128)}), f32[32,16,128]{2,1,0:T(8,128)S(1)}, u32[]{:S(2)}, u32[]{:S(2)}) async-start(f32[32,16,128]{2,1,0:T(8,128)} %broadcast_in_dim.5), calls=%async_computation.3 | async-start | bytes 524288 | tf_op jit(solution)/shard_map/all_to_all | solution.py:130

commit v4 on v2

--- a/solution.py
+++ b/solution.py
@@ -8,23 +8,32 @@
 from jax.sharding import PartitionSpec as P
 
 LANES = 128
-
-
-def project_kernel(rank, dest_ref, slab_ref, factor_ref, out_ref, wide_ref):
+GROUP = ("pair", "core")
+
+
+def project_kernel(dest_ref, slab_ref, factor_ref, out_ref, wide_ref):
     cols, width, depth = slab_ref.shape
+    rank = factor_ref.shape[0]
     half = width // 2
+    pitch = width + 1
+    lane = lax.broadcasted_iota(jnp.int32, (cols, LANES), 1)
     flat = slab_ref[...].reshape(cols * width, depth)
-    wide_ref[...] = jnp.dot(flat, factor_ref[...], preferred_element_type=jnp.float32)
-    lane = lax.broadcasted_iota(jnp.int32, (cols, LANES), 1)
+    twice = jnp.concatenate([factor_ref[...], factor_ref[...]], axis=0)
+    wide = lax.dot_general(
+        flat, twice, (((1,), (1,)), ((), ())), preferred_element_type=jnp.float32
+    )
+    for c in range(cols):
+        wide_ref[c * pitch:c * pitch + width, :] = wide[c * width:(c + 1) * width, :]
     for s in range(half):
-        low = wide_ref[pl.ds(s, cols, stride=width), :]
-        high = wide_ref[pl.ds(s + half, cols, stride=width), :]
+        low = wide_ref[pl.ds(s, cols, stride=pitch), :]
+        high = wide_ref[pl.ds(s + half, cols, stride=pitch), :]
         both = jnp.where(lane < rank, low, high)
         out_ref[:, s * LANES:(s + 1) * LANES] = both.astype(out_ref.dtype)
 
 
-def project(slab, factor_pair, rank, dest, width):
+def project(slab, factor, dest, width):
     cols, total_width, depth = slab.shape
+    rank = factor.shape[0]
     block_cols = 16
     out_width = width * rank
     grid_spec = pltpu.PrefetchScalarGridSpec(
@@ -32,13 +41,13 @@
         grid=(cols // block_cols,),
         in_specs=[
             pl.BlockSpec((block_cols, width, depth), lambda c, d: (c, d[0], 0)),
-            pl.BlockSpec(factor_pair.shape, lambda c, d: (0, 0)),
+            pl.BlockSpec(factor.shape, lambda c, d: (0, 0)),
         ],
         out_specs=pl.BlockSpec((block_cols, out_width), lambda c, d: (c, 0)),
-        scratch_shapes=[pltpu.VMEM((block_cols * width, LANES), jnp.float32)],
+        scratch_shapes=[pltpu.VMEM((block_cols * (width + 1) + 8, LANES), jnp.float32)],
     )
     return pl.pallas_call(
-        functools.partial(project_kernel, rank),
+        project_kernel,
         out_shape=jax.ShapeDtypeStruct((cols, out_width), jnp.bfloat16),
         grid_spec=grid_spec,
         compiler_params=pltpu.CompilerParams(vmem_limit_bytes=44 * 2**20),
@@ -48,7 +57,7 @@
             transcendentals=0,
         ),
         name="project",
-    )(dest.reshape(1), slab, factor_pair)
+    )(dest.reshape(1), slab, factor)
 
 
 def upper_blocks(count):
@@ -100,18 +109,29 @@
     )(places, *pieces)
 
 
-def reduce_scatter(x, axis):
-    n = lax.axis_size(axis)
-    shares = x.reshape(n, x.shape[0] // n, LANES)
-    return lax.all_to_all(shares, axis, split_axis=0, concat_axis=0, tiled=True).sum(axis=0)
-
-
-def gather(x, axis):
-    n = lax.axis_size(axis)
-    copies = jnp.broadcast_to(x[None], (n, *x.shape))
-    return lax.all_to_all(copies, axis, split_axis=0, concat_axis=0, tiled=True).reshape(
-        n * x.shape[0], LANES
-    )
+CHIPS = ("pair", "dev")
+
+
+def exchange(x):
+    return lax.all_to_all(x, CHIPS, split_axis=0, concat_axis=0, tiled=True)
+
+
+def swap_cores(x):
+    return lax.ppermute(x, "core", [(0, 1), (1, 0)])
+
+
+def summed_halves(part):
+    chips = lax.axis_size(CHIPS)
+    core = lax.axis_index("core")
+    rows = part.shape[0]
+    part = jnp.pad(part, ((0, -rows % (16 * chips)), (0, 0)))
+    half = part.shape[0] // 2
+    theirs = lax.dynamic_slice_in_dim(part, (1 - core) * half, half)
+    mine = lax.dynamic_slice_in_dim(part, core * half, half)
+    mine = mine + swap_cores(theirs)
+    share = exchange(mine.reshape(chips, half // chips, LANES)).sum(axis=0)
+    mine = exchange(jnp.broadcast_to(share[None], (chips, *share.shape))).reshape(half, LANES)
+    return mine, swap_cores(mine)
 
 
 def spread_lane(rows, lane):
@@ -169,7 +189,7 @@
     return tri_rows, inv_rows
 
 
-def triangle_kernel(count, place_ref, blocks_ref, out_ref, work_ref, tri_ref, inv_ref):
+def triangle_kernel(count, place_ref, mine_ref, other_ref, out_ref, work_ref, tri_ref, inv_ref):
     step = 8
     high = lax.Precision.HIGHEST
     where = {ab: n for n, ab in enumerate(upper_blocks(count))}
@@ -177,7 +197,11 @@
     def at(a, b):
         return pl.ds(where[a, b] * LANES, LANES)
 
-    work_ref[...] = blocks_ref[:len(where) * LANES, :]
+    half = mine_ref.shape[0]
+    first_core = place_ref[2] == 0
+    work_ref[:half, :] = jnp.where(first_core, mine_ref[...], other_ref[...])
+    left = len(where) * LANES - half
+    work_ref[half:, :] = jnp.where(first_core, other_ref[:left, :], mine_ref[:left, :])
     tri_ref[...] = jnp.zeros_like(tri_ref)
     for p in range(count):
         tri_rows, inv_rows = factor_block(work_ref[at(p, p), :], step)
@@ -201,17 +225,18 @@
     out_ref[...] = tri_ref[pl.ds(row, out_rows), pl.ds(col, LANES)]
 
 
-def own_triangle(blocks, order):
+def own_triangle(mine, other, order):
     row_count = order // lax.axis_size("dev")
-    col_count = order // lax.axis_size("grp")
-    grp = lax.axis_index("grp")
-    place = jnp.stack([lax.axis_index("dev"), grp * col_count // LANES]).astype(jnp.int32)
+    col_count = order // lax.axis_size(GROUP)
+    grp = lax.axis_index(GROUP)
+    place = [lax.axis_index("dev"), grp * col_count // LANES, lax.axis_index("core")]
+    place = jnp.stack(place).astype(jnp.int32)
     count = order // LANES
     rows = len(upper_blocks(count)) * LANES
     out = pl.pallas_call(
         functools.partial(triangle_kernel, count),
         out_shape=jax.ShapeDtypeStruct((row_count, LANES), jnp.float32),
-        in_specs=[pl.BlockSpec(memory_space=pltpu.SMEM), pl.BlockSpec(memory_space=pltpu.VMEM)],
+        in_specs=[pl.BlockSpec(memory_space=pltpu.SMEM)] + [pl.BlockSpec(memory_space=pltpu.VMEM)] * 2,
         out_specs=pl.BlockSpec(memory_space=pltpu.VMEM),
         scratch_shapes=[
             pltpu.VMEM((rows, LANES), jnp.float32),
@@ -223,7 +248,7 @@
             flops=order**3, bytes_accessed=4 * order * order, transcendentals=order
         ),
         name="triangle",
-    )(place, blocks)
+    )(place, mine, other)
     if col_count == LANES:
         return out
     return lax.dynamic_slice(out, (0, grp * col_count % LANES), (row_count, col_count))
@@ -233,35 +258,36 @@
     depth, cols, slab_depth, species = tensor_slab.shape
     rank = mode_factor.shape[1]
     n_dev = lax.axis_size("dev")
-    n_grp = lax.axis_size("grp")
+    n_grp = lax.axis_size(GROUP)
     me = lax.axis_index("dev")
     slab = tensor_slab.transpose(1, 2, 3, 0).reshape(cols, slab_depth * species, depth)
     width = slab_depth * species // n_dev
-    factor_pair = jnp.concatenate([mode_factor, mode_factor], axis=1)
+    factor = mode_factor.T
     pieces, places = [], []
     half = n_dev // 2
     near, far = list(range(1, half)), list(range(half, n_dev))
     order = far[:1] + near[:1] + far[1:2] + near[1:2] + far[2:] + near[2:] + [0]
     for offset in order:
         other = jnp.bitwise_xor(me, offset).astype(jnp.int32)
-        piece = project(slab, factor_pair, rank, other, width)
+        piece = project(slab, factor, other, width)
         if offset:
             piece = lax.ppermute(piece, "dev", [(i, i ^ offset) for i in range(n_dev)])
         pieces.append(piece)
         places.append(other)
     row_total = rank * slab_depth * species * n_grp
     part = gram(pieces, jnp.stack(places), 1.0 / row_total)
-    rows = part.shape[0]
-    unit = 8 * n_dev * n_grp
-    padded = jnp.pad(part, ((0, -rows % unit), (0, 0)))
-    total = reduce_scatter(reduce_scatter(padded, "grp"), "dev")
-    total = gather(gather(total, "dev"), "grp")
-    return own_triangle(total, cols * n_dev)
+    mine, other = summed_halves(part)
+    return own_triangle(mine, other, cols * n_dev)
 
 
 def solution(mesh):
-    in_specs = (P(None, "dev", "grp", None), P())
-    out_specs = P("dev", "grp")
+    cores = 2
+    devices = mesh.devices
+    split = jax.sharding.Mesh(
+        devices.reshape(devices.shape[0] // cores, cores, devices.shape[1]), (*GROUP, "dev")
+    )
+    in_specs = (P(None, "dev", GROUP, None), P())
+    out_specs = P("dev", GROUP)
     return jax.shard_map(
-        per_device, mesh=mesh, in_specs=in_specs, out_specs=out_specs, check_vma=False
-    )
+        per_device, mesh=split, in_specs=in_specs, out_specs=out_specs, check_vma=False
+    )

time: 175 us -> 158 us (0.903)
  Pallas kernels: 61.7 us -> 55 us
  starting transfers between devices: 18.8 us -> 13.7 us
  blocking collectives: 42.4 us -> 39.5 us
    all_to_all x1 -> x0, waiting for transfers between devices: 9.94 us -> none  [gather(): lax.all_to_all(copies, axis, split_axis=0, concat_axis=0, tiled=True)]
    pallas_call x8, Pallas kernels: 39.3 us -> 32.7 us  [project(): pl.pallas_call(project_kernel, out_shape=jax.ShapeDtypeStruct((cols, out_...]
    ppermute x7, waiting for transfers between devices: 38.5 us -> 45.1 us  [per_device(): piece = lax.ppermute(piece, 'dev', [(i, i ^ offset) for i in range(n_dev)])]
    all_to_all x1 -> x0, starting transfers between devices: 3.66 us -> none  [gather(): lax.all_to_all(copies, axis, split_axis=0, concat_axis=0, tiled=True)]
    ppermute x0 -> x2, waiting for transfers between devices: none -> 3.16 us  [swap_cores(): return lax.ppermute(x, 'core', [(0, 1), (1, 0)])]
    all_to_all x3 -> x2, blocking collectives: 42.4 us -> 39.5 us  [exchange(): return lax.all_to_all(x, CHIPS, split_axis=0, concat_axis=0, tiled=True)]
  transfers between devices with their start and end apart: 8 -> 9, of which waited for: 5 -> 6; matrix products, arithmetic and copies ran while one was open for 0% -> 0% of each run, Pallas kernels for 19% -> 18%
where the time goes in v4:
time: 158 us
  Pallas kernels  55 us (35%)
  waiting for transfers between devices  48.2 us (31%)
  blocking collectives  39.5 us (25%)
  starting transfers between devices  13.7 us (9%)
    ppermute x7, waiting for transfers between devices, per_device(): piece = lax.ppermute(piece, 'dev', [(i, i ^ offset) for i in range(n_dev)])  45.1 us
    all_to_all x2, blocking collectives, exchange(): return lax.all_to_all(x, CHIPS, split_axis=0, concat_axis=0, tiled=True)  39.5 us
    pallas_call x8, Pallas kernels, project(): pl.pallas_call(project_kernel, out_shape=jax.ShapeDtypeStruct((cols, out_...  32.7 us
    pallas_call x1, Pallas kernels, own_triangle(): pl.pallas_call(functools.partial(triangle_kernel, count), out_shape=jax.S...  18.3 us
    ppermute x7, starting transfers between devices, per_device(): piece = lax.ppermute(piece, 'dev', [(i, i ^ offset) for i in range(n_dev)])  13.6 us
    pallas_call x1, Pallas kernels, gram(): pl.pallas_call(functools.partial(gram_kernel, scale, count), out_shape=ja...  3.93 us
    ppermute x2, waiting for transfers between devices, swap_cores(): return lax.ppermute(x, 'core', [(0, 1), (1, 0)])  3.16 us
  transfers between devices with their start and end apart: 9, of which 6 were waited for; matrix products, arithmetic and copies ran while one was open for 0% of the time, Pallas kernels for 18%

profile of v4, /device:TPU:0, one launch (start us, length us, event | category | flops | bytes accessed | tf_op | source)
XLA Modules:
  0.0 157.6 jit_solution(8183625709530448312)
XLA Ops:
  0.0 0.8 copy-done
  0.8 4.8 %project.8 = bf16[64,4096]{1,0:T(8,128)(2,1)} custom-call(s32[1]{0:T(128)} %bitcast.3.dest_ref, bf16[64,512,512]{2,1,0:T(8,128)(2,1)} %bitcast.26, bf16[64,512]{1,0:T(8,128)(2,1)S(1)} %bitcast.16), custom_call_target="tpu_custom_call" | custom-call | flops 1073741824 | bytes 4718592 | tf_op jit(solution)/shard_map/project/pallas_call | solution.py:49
  5.6 4.0 %collective-permute-start = (bf16[64,4096]{1,0:T(8,128)(2,1)}, bf16[64,4096]{1,0:T(8,128)(2,1)}, u32[]{:S(2)}, u32[]{:S(2)}) collective-permute-start(bf16[64,4096]{1,0:T(8,128)(2,1)} %project.8), channel_id=1, source_target_pairs={{0,4},{1,5},{2,6},{3,7},{4,0},{5,1},{6,2},{7,3},{8,12},{9,13},{10,... | collective-permute-start | bytes 1572872 | tf_op jit(solution)/shard_map/ppermute | solution.py:274
  9.7 4.0 %project.9 = bf16[64,4096]{1,0:T(8,128)(2,1)S(1)} custom-call(s32[1]{0:T(128)} %bitcast.4.dest_ref, bf16[64,512,512]{2,1,0:T(8,128)(2,1)} %bitcast.27, bf16[64,512]{1,0:T(8,128)(2,1)S(1)} %bitcast.17), custom_call_target="tpu_custom_call" | custom-call | flops 1073741824 | bytes 4718592 | tf_op jit(solution)/shard_map/project/pallas_call | solution.py:49
  13.7 1.6 collective-permute-start.1
  15.2 4.0 %project.10 = bf16[64,4096]{1,0:T(8,128)(2,1)S(1)} custom-call(s32[1]{0:T(128)} %bitcast.5.dest_ref, bf16[64,512,512]{2,1,0:T(8,128)(2,1)} %bitcast.28, bf16[64,512]{1,0:T(8,128)(2,1)S(1)} %bitcast.18), custom_call_target="tpu_custom_call" | custom-call | flops 1073741824 | bytes 4718592 | tf_op jit(solution)/shard_map/project/pallas_call | solution.py:49
  19.2 0.1 collective-permute-start.2
  19.3 4.0 %project.11 = bf16[64,4096]{1,0:T(8,128)(2,1)S(1)} custom-call(s32[1]{0:T(128)} %bitcast.6.dest_ref, bf16[64,512,512]{2,1,0:T(8,128)(2,1)} %bitcast.29, bf16[64,512]{1,0:T(8,128)(2,1)S(1)} %bitcast.19), custom_call_target="tpu_custom_call" | custom-call | flops 1073741824 | bytes 4718592 | tf_op jit(solution)/shard_map/project/pallas_call | solution.py:49
  23.3 1.9 %collective-permute-start.3 = (bf16[64,4096]{1,0:T(8,128)(2,1)S(1)}, bf16[64,4096]{1,0:T(8,128)(2,1)}, u32[]{:S(2)}, u32[]{:S(2)}) collective-permute-start(bf16[64,4096]{1,0:T(8,128)(2,1)S(1)} %project.11), channel_id=1, source_target_pairs={{0,2},{1,3},{2,0},{3,1},{4,6},{5,7},{6,4},{7,5},{8,10},{9,11},{10,... | collective-permute-start | bytes 1572872 | tf_op jit(solution)/shard_map/ppermute | solution.py:274
  25.2 4.0 %project.12 = bf16[64,4096]{1,0:T(8,128)(2,1)S(1)} custom-call(s32[1]{0:T(128)} %bitcast.7.dest_ref, bf16[64,512,512]{2,1,0:T(8,128)(2,1)} %bitcast.30, bf16[64,512]{1,0:T(8,128)(2,1)S(1)} %bitcast.20), custom_call_target="tpu_custom_call" | custom-call | flops 1073741824 | bytes 4718592 | tf_op jit(solution)/shard_map/project/pallas_call | solution.py:49
  29.2 2.5 %collective-permute-start.4 = (bf16[64,4096]{1,0:T(8,128)(2,1)S(1)}, bf16[64,4096]{1,0:T(8,128)(2,1)}, u32[]{:S(2)}, u32[]{:S(2)}) collective-permute-start(bf16[64,4096]{1,0:T(8,128)(2,1)S(1)} %project.12), channel_id=1, source_target_pairs={{0,6},{1,7},{2,4},{3,5},{4,2},{5,3},{6,0},{7,1},{8,14},{9,15},{10,... | collective-permute-start | bytes 1572872 | tf_op jit(solution)/shard_map/ppermute | solution.py:274
  31.7 4.0 %project.13 = bf16[64,4096]{1,0:T(8,128)(2,1)S(1)} custom-call(s32[1]{0:T(128)} %bitcast.8.dest_ref, bf16[64,512,512]{2,1,0:T(8,128)(2,1)} %bitcast.31, bf16[64,512]{1,0:T(8,128)(2,1)S(1)} %bitcast.21), custom_call_target="tpu_custom_call" | custom-call | flops 1073741824 | bytes 4718592 | tf_op jit(solution)/shard_map/project/pallas_call | solution.py:49
  35.7 4.0 %project.14 = bf16[64,4096]{1,0:T(8,128)(2,1)S(1)} custom-call(s32[1]{0:T(128)} %bitcast.9.dest_ref, bf16[64,512,512]{2,1,0:T(8,128)(2,1)} %bitcast.32, bf16[64,512]{1,0:T(8,128)(2,1)S(1)} %bitcast.22), custom_call_target="tpu_custom_call" | custom-call | flops 1073741824 | bytes 4718592 | tf_op jit(solution)/shard_map/project/pallas_call | solution.py:49
  39.7 7.1 %collective-permute-done.refs_0_ = bf16[64,4096]{1,0:T(8,128)(2,1)} collective-permute-done((bf16[64,4096]{1,0:T(8,128)(2,1)}, bf16[64,4096]{1,0:T(8,128)(2,1)}, u32[]{:S(2)}, u32[]{:S(2)}) %collective-permute-start) | collective-permute-done | bytes 524320 | tf_op jit(solution)/shard_map/ppermute | solution.py:274
  46.8 3.5 %collective-permute-start.5 = (bf16[64,4096]{1,0:T(8,128)(2,1)S(1)}, bf16[64,4096]{1,0:T(8,128)(2,1)}, u32[]{:S(2)}, u32[]{:S(2)}) collective-permute-start(bf16[64,4096]{1,0:T(8,128)(2,1)S(1)} %project.13), channel_id=1, source_target_pairs={{0,7},{1,6},{2,5},{3,4},{4,3},{5,2},{6,1},{7,0},{8,15},{9,14},{10,... | collective-permute-start | bytes 1572872 | tf_op jit(solution)/shard_map/ppermute | solution.py:274
  50.2 0.0 collective-permute-done.1.refs_1_
  50.2 0.0 collective-permute-start.6
  50.2 0.1 stack.48.place_ref
  50.3 4.0 %project.15.refs_7_ = bf16[64,4096]{1,0:T(8,128)(2,1)S(1)} custom-call(s32[1]{0:T(128)} %bitcast.dest_ref, bf16[64,512,512]{2,1,0:T(8,128)(2,1)} %bitcast.33, bf16[64,512]{1,0:T(8,128)(2,1)S(1)} %bitcast.23), custom_call_target="tpu_custom_call" | custom-call | flops 1073741824 | bytes 4718592 | tf_op jit(solution)/shard_map/project/pallas_call | solution.py:49
  54.3 25.9 %collective-permute-done.2.refs_2_ = bf16[64,4096]{1,0:T(8,128)(2,1)} collective-permute-done((bf16[64,4096]{1,0:T(8,128)(2,1)S(1)}, bf16[64,4096]{1,0:T(8,128)(2,1)}, u32[]{:S(2)}, u32[]{:S(2)}) %collective-permute-start.2) | collective-permute-done | bytes 524320 | tf_op jit(solution)/shard_map/ppermute | solution.py:274
  80.3 1.8 %collective-permute-done.3.refs_3_ = bf16[64,4096]{1,0:T(8,128)(2,1)} collective-permute-done((bf16[64,4096]{1,0:T(8,128)(2,1)S(1)}, bf16[64,4096]{1,0:T(8,128)(2,1)}, u32[]{:S(2)}, u32[]{:S(2)}) %collective-permute-start.3) | collective-permute-done | bytes 524320 | tf_op jit(solution)/shard_map/ppermute | solution.py:274
  82.0 0.0 collective-permute-done.4.refs_4_
  82.0 0.0 collective-permute-done.5.refs_5_
  82.0 10.3 %collective-permute-done.6.refs_6_ = bf16[64,4096]{1,0:T(8,128)(2,1)S(1)} collective-permute-done((bf16[64,4096]{1,0:T(8,128)(2,1)S(1)}, bf16[64,4096]{1,0:T(8,128)(2,1)S(1)}, u32[]{:S(2)}, u32[]{:S(2)}) %collective-permute-start.6) | collective-permute-done | bytes 524320 | tf_op jit(solution)/shard_map/ppermute | solution.py:274
  92.3 3.9 %gram.1 = f32[1280,128]{1,0:T(8,128)S(1)} custom-call(s32[8]{0:T(128)S(1)} %stack.48.place_ref, bf16[64,4096]{1,0:T(8,128)(2,1)} %collective-permute-done.refs_0_, bf16[64,4096]{1,0:T(8,128)(2,1)} %collective-permute-done.1.refs_1_, bf16[64,4096]{1,0:T(8,128)(2,1)} %collective-permute-done.2.refs_2_, bf16[64,4096]{1,0:T(8,128)(2,1)} %collective-permute-done.3.refs_3_, ...), custom_call_target="tpu_custom_call" | custom-call | flops 2147483648 | bytes 4849664 | tf_op jit(solution)/shard_map/gram/pallas_call | solution.py:95
  96.3 0.1 collective-permute-start.7
  96.4 1.6 %collective-permute-done.7 = f32[640,128]{1,0:T(8,128)S(1)} collective-permute-done((f32[640,128]{1,0:T(8,128)S(1)}, f32[640,128]{1,0:T(8,128)S(1)}, u32[]{:S(2)}, u32[]{:S(2)}) %collective-permute-start.7) | collective-permute-done | bytes 327712 | tf_op jit(solution)/shard_map/ppermute | solution.py:120
  98.0 25.6 %all_to_all.10 = f32[16,40,128]{2,1,0:T(8,128)S(1)} all-to-all(f32[16,40,128]{2,1,0:T(8,128)S(1)} %bitcast.34), channel_id=1, replica_groups=mesh['pair'=2,'core'=2,'dev'=8] {'pair','dev'}, dimensions={0} | all-to-all | bytes 655360 | tf_op jit(solution)/shard_map/all_to_all | solution.py:116
  123.7 13.9 %all_to_all.11 = f32[16,40,128]{2,1,0:T(8,128)S(1)} all-to-all(f32[16,40,128]{2,1,0:T(8,128)S(1)} %broadcast_in_dim.2), channel_id=1, replica_groups=mesh['pair'=2,'core'=2,'dev'=8] {'pair','dev'}, dimensions={0} | all-to-all | bytes 655360 | tf_op jit(solution)/shard_map/all_to_all | solution.py:116
  137.6 0.1 pad_add_fusion.place_ref
  137.7 1.6 collective-permute-done.8.other_ref
  139.2 18.3 %triangle.1 = f32[64,128]{1,0:T(8,128)} custom-call(s32[3]{0:T(128)S(1)} %pad_add_fusion.place_ref, f32[640,128]{1,0:T(8,128)S(1)} %bitcast.25, f32[640,128]{1,0:T(8,128)S(1)} %collective-permute-done.8.other_ref), custom_call_target="tpu_custom_call" | custom-call | flops 134217728 | bytes 1048576 | tf_op jit(solution)/shard_map/triangle/pallas_call | solution.py:236
  (8 shorter events, 0.1 us)
Async XLA Ops:
  0.0 0.8 copy-start
  0.8 8.8 %copy-start.1 = (bf16[512,64]{0,1:T(8,128)(2,1)S(1)}, bf16[512,64]{0,1:T(8,128)(2,1)}, u32[]{:S(2)}) copy-start(bf16[512,64]{0,1:T(8,128)(2,1)} %param.3) | copy-start | bytes 196612
  5.6 41.1 %collective-permute-start = (bf16[64,4096]{1,0:T(8,128)(2,1)}, bf16[64,4096]{1,0:T(8,128)(2,1)}, u32[]{:S(2)}, u32[]{:S(2)}) collective-permute-start(bf16[64,4096]{1,0:T(8,128)(2,1)} %project.8), channel_id=1, source_target_pairs={{0,4},{1,5},{2,6},{3,7},{4,0},{5,1},{6,2},{7,3},{8,12},{9,13},{10,... | collective-permute-start | bytes 1572872 | tf_op jit(solution)/shard_map/ppermute | solution.py:274
  13.7 36.6 %collective-permute-start.1 = (bf16[64,4096]{1,0:T(8,128)(2,1)S(1)}, bf16[64,4096]{1,0:T(8,128)(2,1)}, u32[]{:S(2)}, u32[]{:S(2)}) collective-permute-start(bf16[64,4096]{1,0:T(8,128)(2,1)S(1)} %project.9), channel_id=1, source_target_pairs={{0,1},{1,0},{2,3},{3,2},{4,5},{5,4},{6,7},{7,6},{8,9},{9,8},{10,11... | collective-permute-start | bytes 1572872 | tf_op jit(solution)/shard_map/ppermute | solution.py:274
  19.2 61.0 %collective-permute-start.2 = (bf16[64,4096]{1,0:T(8,128)(2,1)S(1)}, bf16[64,4096]{1,0:T(8,128)(2,1)}, u32[]{:S(2)}, u32[]{:S(2)}) collective-permute-start(bf16[64,4096]{1,0:T(8,128)(2,1)S(1)} %project.10), channel_id=1, source_target_pairs={{0,5},{1,4},{2,7},{3,6},{4,1},{5,0},{6,3},{7,2},{8,13},{9,12},{10,... | collective-permute-start | bytes 1572872 | tf_op jit(solution)/shard_map/ppermute | solution.py:274
  23.3 58.7 %collective-permute-start.3 = (bf16[64,4096]{1,0:T(8,128)(2,1)S(1)}, bf16[64,4096]{1,0:T(8,128)(2,1)}, u32[]{:S(2)}, u32[]{:S(2)}) collective-permute-start(bf16[64,4096]{1,0:T(8,128)(2,1)S(1)} %project.11), channel_id=1, source_target_pairs={{0,2},{1,3},{2,0},{3,1},{4,6},{5,7},{6,4},{7,5},{8,10},{9,11},{10,... | collective-permute-start | bytes 1572872 | tf_op jit(solution)/shard_map/ppermute | solution.py:274
  29.2 52.9 %collective-permute-start.4 = (bf16[64,4096]{1,0:T(8,128)(2,1)S(1)}, bf16[64,4096]{1,0:T(8,128)(2,1)}, u32[]{:S(2)}, u32[]{:S(2)}) collective-permute-start(bf16[64,4096]{1,0:T(8,128)(2,1)S(1)} %project.12), channel_id=1, source_target_pairs={{0,6},{1,7},{2,4},{3,5},{4,2},{5,3},{6,0},{7,1},{8,14},{9,15},{10,... | collective-permute-start | bytes 1572872 | tf_op jit(solution)/shard_map/ppermute | solution.py:274
  46.8 35.3 %collective-permute-start.5 = (bf16[64,4096]{1,0:T(8,128)(2,1)S(1)}, bf16[64,4096]{1,0:T(8,128)(2,1)}, u32[]{:S(2)}, u32[]{:S(2)}) collective-permute-start(bf16[64,4096]{1,0:T(8,128)(2,1)S(1)} %project.13), channel_id=1, source_target_pairs={{0,7},{1,6},{2,5},{3,4},{4,3},{5,2},{6,1},{7,0},{8,15},{9,14},{10,... | collective-permute-start | bytes 1572872 | tf_op jit(solution)/shard_map/ppermute | solution.py:274
  50.2 42.1 %collective-permute-start.6 = (bf16[64,4096]{1,0:T(8,128)(2,1)S(1)}, bf16[64,4096]{1,0:T(8,128)(2,1)S(1)}, u32[]{:S(2)}, u32[]{:S(2)}) collective-permute-start(bf16[64,4096]{1,0:T(8,128)(2,1)S(1)} %project.14), channel_id=1, source_target_pairs={{0,3},{1,2},{2,1},{3,0},{4,7},{5,6},{6,5},{7,4},{8,11},{9,10},{10,... | collective-permute-start | bytes 1572872 | tf_op jit(solution)/shard_map/ppermute | solution.py:274
  96.3 1.7 %collective-permute-start.7 = (f32[640,128]{1,0:T(8,128)S(1)}, f32[640,128]{1,0:T(8,128)S(1)}, u32[]{:S(2)}, u32[]{:S(2)}) collective-permute-start(f32[640,128]{1,0:T(8,128)S(1)} %constant_dynamic-slice_fusion), channel_id=1, source_target_pairs={{0,8},{8,0},{1,9},{9,1},{2,10},{10,2},{3,11},{11,3},{4,12},{12,4},... | collective-permute-start | bytes 983048 | tf_op jit(solution)/shard_map/ppermute | solution.py:120
  137.6 1.6 %collective-permute-start.8 = (f32[640,128]{1,0:T(8,128)S(1)}, f32[640,128]{1,0:T(8,128)S(1)}, u32[]{:S(2)}, u32[]{:S(2)}) collective-permute-start(f32[640,128]{1,0:T(8,128)S(1)} %bitcast.24), channel_id=1, source_target_pairs={{0,8},{8,0},{1,9},{9,1},{2,10},{10,2},{3,11},{11,3},{4,12},{12,4},... | collective-permute-start | bytes 983048 | tf_op jit(solution)/shard_map/ppermute | solution.py:120

commit v5 on v4

--- a/solution.py
+++ b/solution.py
@@ -31,16 +31,17 @@
         out_ref[:, s * LANES:(s + 1) * LANES] = both.astype(out_ref.dtype)
 
 
-def project(slab, factor, dest, width):
-    cols, total_width, depth = slab.shape
+def project(slab, factor, dest, width, first, cols):
+    depth = slab.shape[2]
     rank = factor.shape[0]
     block_cols = 16
+    first_block = first // block_cols
     out_width = width * rank
     grid_spec = pltpu.PrefetchScalarGridSpec(
         num_scalar_prefetch=1,
         grid=(cols // block_cols,),
         in_specs=[
-            pl.BlockSpec((block_cols, width, depth), lambda c, d: (c, d[0], 0)),
+            pl.BlockSpec((block_cols, width, depth), lambda c, d: (first_block + c, d[0], 0)),
             pl.BlockSpec(factor.shape, lambda c, d: (0, 0)),
         ],
         out_specs=pl.BlockSpec((block_cols, out_width), lambda c, d: (c, 0)),
@@ -67,11 +68,10 @@
 def gram_kernel(scale, count, place_ref, *refs):
     pieces = refs[:count]
     out_ref, full_ref = refs[count:]
-    cols = pieces[0].shape[0]
     for i, piece in enumerate(pieces):
-        start = pl.multiple_of(place_ref[i] * cols, 16)
-        full_ref[pl.ds(start, cols), :] = piece[...]
-    order = cols * count
+        start = pl.multiple_of(place_ref[i], 16)
+        full_ref[pl.ds(start, piece.shape[0]), :] = piece[...]
+    order = full_ref.shape[0]
     where = {ab: n for n, ab in enumerate(upper_blocks(order // LANES))}
     wide = 2 * LANES
     for tile in range(order // wide):
@@ -88,9 +88,9 @@
 
 
 def gram(pieces, places, scale):
-    cols, width = pieces[0].shape
+    width = pieces[0].shape[1]
     count = len(pieces)
-    order = cols * count
+    order = sum(piece.shape[0] for piece in pieces)
     rows = len(upper_blocks(order // LANES)) * LANES
     return pl.pallas_call(
         functools.partial(gram_kernel, scale, count),
@@ -192,33 +192,41 @@
 def triangle_kernel(count, place_ref, mine_ref, other_ref, out_ref, work_ref, tri_ref, inv_ref):
     step = 8
     high = lax.Precision.HIGHEST
-    where = {ab: n for n, ab in enumerate(upper_blocks(count))}
-
-    def at(a, b):
-        return pl.ds(where[a, b] * LANES, LANES)
-
     half = mine_ref.shape[0]
     first_core = place_ref[2] == 0
-    work_ref[:half, :] = jnp.where(first_core, mine_ref[...], other_ref[...])
-    left = len(where) * LANES - half
-    work_ref[half:, :] = jnp.where(first_core, other_ref[:left, :], mine_ref[:left, :])
+    order = count * LANES
+
+    def rows(a):
+        return slice(a * LANES, (a + 1) * LANES)
+
+    def take_off(p, a, first, last):
+        work_ref[rows(a), first:last] -= lax.dot_general(
+            tri_ref[rows(p), rows(a)], tri_ref[rows(p), first:last],
+            (((0,), (0,)), ((), ())), precision=high, preferred_element_type=jnp.float32,
+        )
+
+    for n, (a, b) in enumerate(upper_blocks(count)):
+        at = n * LANES % half
+        near, far = (mine_ref, other_ref) if n * LANES < half else (other_ref, mine_ref)
+        work_ref[rows(a), rows(b)] = jnp.where(first_core, near[at:at + LANES, :], far[at:at + LANES, :])
     tri_ref[...] = jnp.zeros_like(tri_ref)
     for p in range(count):
-        tri_rows, inv_rows = factor_block(work_ref[at(p, p), :], step)
+        tri_rows, inv_rows = factor_block(work_ref[rows(p), rows(p)], step)
         for i in range(LANES // step):
-            tri_ref[p * LANES + i * step:p * LANES + (i + 1) * step, p * LANES:(p + 1) * LANES] = tri_rows[i]
+            at = slice(p * LANES + i * step, p * LANES + (i + 1) * step)
+            tri_ref[at, rows(p)] = tri_rows[i]
             inv_ref[i * step:(i + 1) * step, :] = inv_rows[i]
-        for q in range(p + 1, count):
-            tri_ref[p * LANES:(p + 1) * LANES, q * LANES:(q + 1) * LANES] = jnp.dot(
-                inv_ref[...], work_ref[at(p, q), :], precision=high, preferred_element_type=jnp.float32
-            )
-        for a in range(p + 1, count):
-            for b in range(a, count):
-                work_ref[at(a, b), :] -= lax.dot_general(
-                    tri_ref[p * LANES:(p + 1) * LANES, a * LANES:(a + 1) * LANES],
-                    tri_ref[p * LANES:(p + 1) * LANES, b * LANES:(b + 1) * LANES],
-                    (((0,), (0,)), ((), ())), precision=high, preferred_element_type=jnp.float32,
-                )
+        if p + 1 == count:
+            break
+        after = (p + 1) * LANES
+        tri_ref[rows(p), after:] = jnp.dot(
+            inv_ref[...], work_ref[rows(p), after:], precision=high, preferred_element_type=jnp.float32
+        )
+        take_off(p, p + 1, after, after + LANES)
+        if after + LANES < order:
+            take_off(p, p + 1, after + LANES, order)
+        for a in range(p + 2, count):
+            take_off(p, a, a * LANES, order)
     out_rows = out_ref.shape[0]
     row = pl.multiple_of(place_ref[0] * out_rows, 8)
     col = pl.multiple_of(place_ref[1] * LANES, LANES)
@@ -232,14 +240,13 @@
     place = [lax.axis_index("dev"), grp * col_count // LANES, lax.axis_index("core")]
     place = jnp.stack(place).astype(jnp.int32)
     count = order // LANES
-    rows = len(upper_blocks(count)) * LANES
     out = pl.pallas_call(
         functools.partial(triangle_kernel, count),
         out_shape=jax.ShapeDtypeStruct((row_count, LANES), jnp.float32),
         in_specs=[pl.BlockSpec(memory_space=pltpu.SMEM)] + [pl.BlockSpec(memory_space=pltpu.VMEM)] * 2,
         out_specs=pl.BlockSpec(memory_space=pltpu.VMEM),
         scratch_shapes=[
-            pltpu.VMEM((rows, LANES), jnp.float32),
+            pltpu.VMEM((order, order), jnp.float32),
             pltpu.VMEM((order, order), jnp.float32),
             pltpu.VMEM((LANES, LANES), jnp.float32),
         ],
@@ -269,11 +276,13 @@
     order = far[:1] + near[:1] + far[1:2] + near[1:2] + far[2:] + near[2:] + [0]
     for offset in order:
         other = jnp.bitwise_xor(me, offset).astype(jnp.int32)
-        piece = project(slab, factor, other, width)
-        if offset:
-            piece = lax.ppermute(piece, "dev", [(i, i ^ offset) for i in range(n_dev)])
-        pieces.append(piece)
-        places.append(other)
+        cuts = 2 if offset == half and cols % 32 == 0 else 1
+        for first in range(0, cols, cols // cuts):
+            piece = project(slab, factor, other, width, first, cols // cuts)
+            if offset:
+                piece = lax.ppermute(piece, "dev", [(i, i ^ offset) for i in range(n_dev)])
+            pieces.append(piece)
+            places.append(other * cols + first)
     row_total = rank * slab_depth * species * n_grp
     part = gram(pieces, jnp.stack(places), 1.0 / row_total)
     mine, other = summed_halves(part)

time: 158 us -> 156 us (0.987)
  waiting for transfers between devices: 48.2 us -> 46 us
    ppermute x7 -> x8, waiting for transfers between devices: 45.1 us -> 42.8 us  [per_device(): piece = lax.ppermute(piece, 'dev', [(i, i ^ offset) for i in range(n_dev)])]
    ppermute x7 -> x8, starting transfers between devices: 13.6 us -> 14.3 us  [per_device(): piece = lax.ppermute(piece, 'dev', [(i, i ^ offset) for i in range(n_dev)])]
    pallas_call x8 -> x9, Pallas kernels: 32.7 us -> 32.9 us  [project(): pl.pallas_call(project_kernel, out_shape=jax.ShapeDtypeStruct((cols, out_...]
  transfers between devices with their start and end apart: 9 -> 10, of which waited for: 6 -> 6; matrix products, arithmetic and copies ran while one was open for 0% -> 0% of each run, Pallas kernels for 18% -> 20%
where the time goes in v5:
time: 156 us; the launch traced here: 155 us
  Pallas kernels  55.5 us (36%)
  waiting for transfers between devices  46 us (29%)
  blocking collectives  38.1 us (24%)
  starting transfers between devices  14.4 us (9%)
    ppermute x8, waiting for transfers between devices, per_device(): piece = lax.ppermute(piece, 'dev', [(i, i ^ offset) for i in range(n_dev)])  42.8 us
    all_to_all x2, blocking collectives, exchange(): return lax.all_to_all(x, CHIPS, split_axis=0, concat_axis=0, tiled=True)  38.1 us
    pallas_call x9, Pallas kernels, project(): pl.pallas_call(project_kernel, out_shape=jax.ShapeDtypeStruct((cols, out_...  32.9 us
    pallas_call x1, Pallas kernels, own_triangle(): pl.pallas_call(functools.partial(triangle_kernel, count), out_shape=jax.S...  18.7 us
    ppermute x8, starting transfers between devices, per_device(): piece = lax.ppermute(piece, 'dev', [(i, i ^ offset) for i in range(n_dev)])  14.3 us
    pallas_call x1, Pallas kernels, gram(): pl.pallas_call(functools.partial(gram_kernel, scale, count), out_shape=ja...  3.93 us
    ppermute x2, waiting for transfers between devices, swap_cores(): return lax.ppermute(x, 'core', [(0, 1), (1, 0)])  3.16 us
  transfers between devices with their start and end apart: 10, of which 6 were waited for; matrix products, arithmetic and copies ran while one was open for 0% of the time, Pallas kernels for 20%

profile of v5, /device:TPU:0, one launch (start us, length us, event | category | flops | bytes accessed | tf_op | source)
XLA Modules:
  0.0 155.2 jit_solution(18407861486496392898)
XLA Ops:
  0.0 0.8 copy-done
  0.8 2.2 %project.9 = bf16[32,4096]{1,0:T(8,128)(2,1)S(1)} custom-call(s32[1]{0:T(128)} %bitcast.12.dest_ref, bf16[64,512,512]{2,1,0:T(8,128)(2,1)} %bitcast.36, bf16[64,512]{1,0:T(8,128)(2,1)S(1)} %bitcast.25), custom_call_target="tpu_custom_call" | custom-call | flops 536870912 | bytes 2359296 | tf_op jit(solution)/shard_map/project/pallas_call | solution.py:50
  3.1 4.1 %collective-permute-start = (bf16[32,4096]{1,0:T(8,128)(2,1)S(1)}, bf16[32,4096]{1,0:T(8,128)(2,1)}, u32[]{:S(2)}, u32[]{:S(2)}) collective-permute-start(bf16[32,4096]{1,0:T(8,128)(2,1)S(1)} %project.9), channel_id=1, source_target_pairs={{0,4},{1,5},{2,6},{3,7},{4,0},{5,1},{6,2},{7,3},{8,12},{9,13},{10,... | collective-permute-start | bytes 786440 | tf_op jit(solution)/shard_map/ppermute | solution.py:283
  7.2 4.0 %project.11 = bf16[64,4096]{1,0:T(8,128)(2,1)S(1)} custom-call(s32[1]{0:T(128)} %bitcast.17.dest_ref, bf16[64,512,512]{2,1,0:T(8,128)(2,1)} %bitcast.37, bf16[64,512]{1,0:T(8,128)(2,1)S(1)} %bitcast.26), custom_call_target="tpu_custom_call" | custom-call | flops 1073741824 | bytes 4718592 | tf_op jit(solution)/shard_map/project/pallas_call | solution.py:50
  11.2 1.6 %collective-permute-start.2 = (bf16[64,4096]{1,0:T(8,128)(2,1)S(1)}, bf16[64,4096]{1,0:T(8,128)(2,1)}, u32[]{:S(2)}, u32[]{:S(2)}) collective-permute-start(bf16[64,4096]{1,0:T(8,128)(2,1)S(1)} %project.11), channel_id=1, source_target_pairs={{0,1},{1,0},{2,3},{3,2},{4,5},{5,4},{6,7},{7,6},{8,9},{9,8},{10,11... | collective-permute-start | bytes 1572872 | tf_op jit(solution)/shard_map/ppermute | solution.py:283
  12.8 2.8 %project.10 = bf16[32,4096]{1,0:T(8,128)(2,1)} custom-call(s32[1]{0:T(128)} %bitcast.12.dest_ref, bf16[64,512,512]{2,1,0:T(8,128)(2,1)} %bitcast.38, bf16[64,512]{1,0:T(8,128)(2,1)S(1)} %bitcast.27), custom_call_target="tpu_custom_call" | custom-call | flops 536870912 | bytes 2359296 | tf_op jit(solution)/shard_map/project/pallas_call | solution.py:50
  15.6 0.3 collective-permute-start.1
  15.9 4.0 %project.12 = bf16[64,4096]{1,0:T(8,128)(2,1)S(1)} custom-call(s32[1]{0:T(128)} %bitcast.18.dest_ref, bf16[64,512,512]{2,1,0:T(8,128)(2,1)} %bitcast.39, bf16[64,512]{1,0:T(8,128)(2,1)S(1)} %bitcast.28), custom_call_target="tpu_custom_call" | custom-call | flops 1073741824 | bytes 4718592 | tf_op jit(solution)/shard_map/project/pallas_call | solution.py:50
  19.9 2.6 %collective-permute-start.3 = (bf16[64,4096]{1,0:T(8,128)(2,1)S(1)}, bf16[64,4096]{1,0:T(8,128)(2,1)}, u32[]{:S(2)}, u32[]{:S(2)}) collective-permute-start(bf16[64,4096]{1,0:T(8,128)(2,1)S(1)} %project.12), channel_id=1, source_target_pairs={{0,5},{1,4},{2,7},{3,6},{4,1},{5,0},{6,3},{7,2},{8,13},{9,12},{10,... | collective-permute-start | bytes 1572872 | tf_op jit(solution)/shard_map/ppermute | solution.py:283
  22.5 4.0 %project.13 = bf16[64,4096]{1,0:T(8,128)(2,1)S(1)} custom-call(s32[1]{0:T(128)} %bitcast.19.dest_ref, bf16[64,512,512]{2,1,0:T(8,128)(2,1)} %bitcast.40, bf16[64,512]{1,0:T(8,128)(2,1)S(1)} %bitcast.29), custom_call_target="tpu_custom_call" | custom-call | flops 1073741824 | bytes 4718592 | tf_op jit(solution)/shard_map/project/pallas_call | solution.py:50
  26.5 1.7 %collective-permute-start.4 = (bf16[64,4096]{1,0:T(8,128)(2,1)S(1)}, bf16[64,4096]{1,0:T(8,128)(2,1)}, u32[]{:S(2)}, u32[]{:S(2)}) collective-permute-start(bf16[64,4096]{1,0:T(8,128)(2,1)S(1)} %project.13), channel_id=1, source_target_pairs={{0,2},{1,3},{2,0},{3,1},{4,6},{5,7},{6,4},{7,5},{8,10},{9,11},{10,... | collective-permute-start | bytes 1572872 | tf_op jit(solution)/shard_map/ppermute | solution.py:283
  28.1 4.0 %project.14 = bf16[64,4096]{1,0:T(8,128)(2,1)S(1)} custom-call(s32[1]{0:T(128)} %bitcast.20.dest_ref, bf16[64,512,512]{2,1,0:T(8,128)(2,1)} %bitcast.41, bf16[64,512]{1,0:T(8,128)(2,1)S(1)} %bitcast.30), custom_call_target="tpu_custom_call" | custom-call | flops 1073741824 | bytes 4718592 | tf_op jit(solution)/shard_map/project/pallas_call | solution.py:50
  32.1 4.0 %project.15 = bf16[64,4096]{1,0:T(8,128)(2,1)S(1)} custom-call(s32[1]{0:T(128)} %bitcast.21.dest_ref, bf16[64,512,512]{2,1,0:T(8,128)(2,1)} %bitcast.42, bf16[64,512]{1,0:T(8,128)(2,1)S(1)} %bitcast.31), custom_call_target="tpu_custom_call" | custom-call | flops 1073741824 | bytes 4718592 | tf_op jit(solution)/shard_map/project/pallas_call | solution.py:50
  36.1 4.0 %project.16 = bf16[64,4096]{1,0:T(8,128)(2,1)S(1)} custom-call(s32[1]{0:T(128)} %bitcast.22.dest_ref, bf16[64,512,512]{2,1,0:T(8,128)(2,1)} %bitcast.43, bf16[64,512]{1,0:T(8,128)(2,1)S(1)} %bitcast.32), custom_call_target="tpu_custom_call" | custom-call | flops 1073741824 | bytes 4718592 | tf_op jit(solution)/shard_map/project/pallas_call | solution.py:50
  40.1 0.0 collective-permute-done.refs_0_
  40.1 0.1 collective-permute-start.5
  40.2 2.2 %collective-permute-done.1.refs_1_ = bf16[32,4096]{1,0:T(8,128)(2,1)} collective-permute-done((bf16[32,4096]{1,0:T(8,128)(2,1)}, bf16[32,4096]{1,0:T(8,128)(2,1)}, u32[]{:S(2)}, u32[]{:S(2)}) %collective-permute-start.1) | collective-permute-done | bytes 262176 | tf_op jit(solution)/shard_map/ppermute | solution.py:283
  42.4 4.0 %collective-permute-start.6 = (bf16[64,4096]{1,0:T(8,128)(2,1)S(1)}, bf16[64,4096]{1,0:T(8,128)(2,1)}, u32[]{:S(2)}, u32[]{:S(2)}) collective-permute-start(bf16[64,4096]{1,0:T(8,128)(2,1)S(1)} %project.15), channel_id=1, source_target_pairs={{0,7},{1,6},{2,5},{3,4},{4,3},{5,2},{6,1},{7,0},{8,15},{9,14},{10,... | collective-permute-start | bytes 1572872 | tf_op jit(solution)/shard_map/ppermute | solution.py:283
  46.4 0.0 collective-permute-done.2.refs_2_
  46.4 0.1 stack.55.place_ref
  46.5 4.0 %project.17.refs_8_ = bf16[64,4096]{1,0:T(8,128)(2,1)S(1)} custom-call(s32[1]{0:T(128)} %bitcast.dest_ref, bf16[64,512,512]{2,1,0:T(8,128)(2,1)} %bitcast.44, bf16[64,512]{1,0:T(8,128)(2,1)S(1)} %bitcast.33), custom_call_target="tpu_custom_call" | custom-call | flops 1073741824 | bytes 4718592 | tf_op jit(solution)/shard_map/project/pallas_call | solution.py:50
  50.4 27.1 %collective-permute-done.3.refs_3_ = bf16[64,4096]{1,0:T(8,128)(2,1)} collective-permute-done((bf16[64,4096]{1,0:T(8,128)(2,1)S(1)}, bf16[64,4096]{1,0:T(8,128)(2,1)}, u32[]{:S(2)}, u32[]{:S(2)}) %collective-permute-start.3) | collective-permute-done | bytes 524320 | tf_op jit(solution)/shard_map/ppermute | solution.py:283
  77.6 2.6 %collective-permute-done.4.refs_4_ = bf16[64,4096]{1,0:T(8,128)(2,1)} collective-permute-done((bf16[64,4096]{1,0:T(8,128)(2,1)S(1)}, bf16[64,4096]{1,0:T(8,128)(2,1)}, u32[]{:S(2)}, u32[]{:S(2)}) %collective-permute-start.4) | collective-permute-done | bytes 524320 | tf_op jit(solution)/shard_map/ppermute | solution.py:283
  80.2 10.8 %collective-permute-done.7.refs_7_ = bf16[64,4096]{1,0:T(8,128)(2,1)S(1)} collective-permute-done((bf16[64,4096]{1,0:T(8,128)(2,1)S(1)}, bf16[64,4096]{1,0:T(8,128)(2,1)S(1)}, u32[]{:S(2)}, u32[]{:S(2)}) %collective-permute-start.7) | collective-permute-done | bytes 524320 | tf_op jit(solution)/shard_map/ppermute | solution.py:283
  91.0 3.9 %gram.1 = f32[1280,128]{1,0:T(8,128)S(1)} custom-call(s32[9]{0:T(128)S(1)} %stack.55.place_ref, bf16[32,4096]{1,0:T(8,128)(2,1)} %collective-permute-done.refs_0_, bf16[32,4096]{1,0:T(8,128)(2,1)} %collective-permute-done.1.refs_1_, bf16[64,4096]{1,0:T(8,128)(2,1)} %collective-permute-done.2.refs_2_, bf16[64,4096]{1,0:T(8,128)(2,1)} %collective-permute-done.3.refs_3_, ...), custom_call_target="tpu_custom_call" | custom-call | flops 2147483648 | bytes 4849664 | tf_op jit(solution)/shard_map/gram/pallas_call | solution.py:95
  95.0 0.1 collective-permute-start.8
  95.1 1.6 %collective-permute-done.8 = f32[640,128]{1,0:T(8,128)S(1)} collective-permute-done((f32[640,128]{1,0:T(8,128)S(1)}, f32[640,128]{1,0:T(8,128)S(1)}, u32[]{:S(2)}, u32[]{:S(2)}) %collective-permute-start.8) | collective-permute-done | bytes 327712 | tf_op jit(solution)/shard_map/ppermute | solution.py:120
  96.7 24.2 %all_to_all.10 = f32[16,40,128]{2,1,0:T(8,128)S(1)} all-to-all(f32[16,40,128]{2,1,0:T(8,128)S(1)} %bitcast.45), channel_id=1, replica_groups=mesh['pair'=2,'core'=2,'dev'=8] {'pair','dev'}, dimensions={0} | all-to-all | bytes 655360 | tf_op jit(solution)/shard_map/all_to_all | solution.py:116
  121.0 13.9 %all_to_all.11 = f32[16,40,128]{2,1,0:T(8,128)S(1)} all-to-all(f32[16,40,128]{2,1,0:T(8,128)S(1)} %broadcast_in_dim.2), channel_id=1, replica_groups=mesh['pair'=2,'core'=2,'dev'=8] {'pair','dev'}, dimensions={0} | all-to-all | bytes 655360 | tf_op jit(solution)/shard_map/all_to_all | solution.py:116
  134.9 0.1 pad_add_fusion.place_ref
  135.0 1.6 collective-permute-done.9.other_ref
  136.5 18.7 %triangle.1 = f32[64,128]{1,0:T(8,128)} custom-call(s32[3]{0:T(128)S(1)} %pad_add_fusion.place_ref, f32[640,128]{1,0:T(8,128)S(1)} %bitcast.35, f32[640,128]{1,0:T(8,128)S(1)} %collective-permute-done.9.other_ref), custom_call_target="tpu_custom_call" | custom-call | flops 134217728 | bytes 1048576 | tf_op jit(solution)/shard_map/triangle/pallas_call | solution.py:243
  (11 shorter events, 0.1 us)
Async XLA Ops:
  0.0 0.8 copy-start
  0.8 6.3 %copy-start.1 = (bf16[512,64]{0,1:T(8,128)(2,1)S(1)}, bf16[512,64]{0,1:T(8,128)(2,1)}, u32[]{:S(2)}) copy-start(bf16[512,64]{0,1:T(8,128)(2,1)} %param.3) | copy-start | bytes 196612
  3.1 37.0 %collective-permute-start = (bf16[32,4096]{1,0:T(8,128)(2,1)S(1)}, bf16[32,4096]{1,0:T(8,128)(2,1)}, u32[]{:S(2)}, u32[]{:S(2)}) collective-permute-start(bf16[32,4096]{1,0:T(8,128)(2,1)S(1)} %project.9), channel_id=1, source_target_pairs={{0,4},{1,5},{2,6},{3,7},{4,0},{5,1},{6,2},{7,3},{8,12},{9,13},{10,... | collective-permute-start | bytes 786440 | tf_op jit(solution)/shard_map/ppermute | solution.py:283
  11.2 35.2 %collective-permute-start.2 = (bf16[64,4096]{1,0:T(8,128)(2,1)S(1)}, bf16[64,4096]{1,0:T(8,128)(2,1)}, u32[]{:S(2)}, u32[]{:S(2)}) collective-permute-start(bf16[64,4096]{1,0:T(8,128)(2,1)S(1)} %project.11), channel_id=1, source_target_pairs={{0,1},{1,0},{2,3},{3,2},{4,5},{5,4},{6,7},{7,6},{8,9},{9,8},{10,11... | collective-permute-start | bytes 1572872 | tf_op jit(solution)/shard_map/ppermute | solution.py:283
  15.6 26.8 %collective-permute-start.1 = (bf16[32,4096]{1,0:T(8,128)(2,1)}, bf16[32,4096]{1,0:T(8,128)(2,1)}, u32[]{:S(2)}, u32[]{:S(2)}) collective-permute-start(bf16[32,4096]{1,0:T(8,128)(2,1)} %project.10), channel_id=1, source_target_pairs={{0,4},{1,5},{2,6},{3,7},{4,0},{5,1},{6,2},{7,3},{8,12},{9,13},{10,... | collective-permute-start | bytes 786440 | tf_op jit(solution)/shard_map/ppermute | solution.py:283
  19.9 57.7 %collective-permute-start.3 = (bf16[64,4096]{1,0:T(8,128)(2,1)S(1)}, bf16[64,4096]{1,0:T(8,128)(2,1)}, u32[]{:S(2)}, u32[]{:S(2)}) collective-permute-start(bf16[64,4096]{1,0:T(8,128)(2,1)S(1)} %project.12), channel_id=1, source_target_pairs={{0,5},{1,4},{2,7},{3,6},{4,1},{5,0},{6,3},{7,2},{8,13},{9,12},{10,... | collective-permute-start | bytes 1572872 | tf_op jit(solution)/shard_map/ppermute | solution.py:283
  26.5 53.7 %collective-permute-start.4 = (bf16[64,4096]{1,0:T(8,128)(2,1)S(1)}, bf16[64,4096]{1,0:T(8,128)(2,1)}, u32[]{:S(2)}, u32[]{:S(2)}) collective-permute-start(bf16[64,4096]{1,0:T(8,128)(2,1)S(1)} %project.13), channel_id=1, source_target_pairs={{0,2},{1,3},{2,0},{3,1},{4,6},{5,7},{6,4},{7,5},{8,10},{9,11},{10,... | collective-permute-start | bytes 1572872 | tf_op jit(solution)/shard_map/ppermute | solution.py:283
  40.1 40.1 %collective-permute-start.5 = (bf16[64,4096]{1,0:T(8,128)(2,1)S(1)}, bf16[64,4096]{1,0:T(8,128)(2,1)}, u32[]{:S(2)}, u32[]{:S(2)}) collective-permute-start(bf16[64,4096]{1,0:T(8,128)(2,1)S(1)} %project.14), channel_id=1, source_target_pairs={{0,6},{1,7},{2,4},{3,5},{4,2},{5,3},{6,0},{7,1},{8,14},{9,15},{10,... | collective-permute-start | bytes 1572872 | tf_op jit(solution)/shard_map/ppermute | solution.py:283
  42.4 37.8 %collective-permute-start.6 = (bf16[64,4096]{1,0:T(8,128)(2,1)S(1)}, bf16[64,4096]{1,0:T(8,128)(2,1)}, u32[]{:S(2)}, u32[]{:S(2)}) collective-permute-start(bf16[64,4096]{1,0:T(8,128)(2,1)S(1)} %project.15), channel_id=1, source_target_pairs={{0,7},{1,6},{2,5},{3,4},{4,3},{5,2},{6,1},{7,0},{8,15},{9,14},{10,... | collective-permute-start | bytes 1572872 | tf_op jit(solution)/shard_map/ppermute | solution.py:283
  46.4 44.7 %collective-permute-start.7 = (bf16[64,4096]{1,0:T(8,128)(2,1)S(1)}, bf16[64,4096]{1,0:T(8,128)(2,1)S(1)}, u32[]{:S(2)}, u32[]{:S(2)}) collective-permute-start(bf16[64,4096]{1,0:T(8,128)(2,1)S(1)} %project.16), channel_id=1, source_target_pairs={{0,3},{1,2},{2,1},{3,0},{4,7},{5,6},{6,5},{7,4},{8,11},{9,10},{10,... | collective-permute-start | bytes 1572872 | tf_op jit(solution)/shard_map/ppermute | solution.py:283
  95.0 1.7 %collective-permute-start.8 = (f32[640,128]{1,0:T(8,128)S(1)}, f32[640,128]{1,0:T(8,128)S(1)}, u32[]{:S(2)}, u32[]{:S(2)}) collective-permute-start(f32[640,128]{1,0:T(8,128)S(1)} %constant_dynamic-slice_fusion), channel_id=1, source_target_pairs={{0,8},{8,0},{1,9},{9,1},{2,10},{10,2},{3,11},{11,3},{4,12},{12,4},... | collective-permute-start | bytes 983048 | tf_op jit(solution)/shard_map/ppermute | solution.py:120
  134.9 1.6 %collective-permute-start.9 = (f32[640,128]{1,0:T(8,128)S(1)}, f32[640,128]{1,0:T(8,128)S(1)}, u32[]{:S(2)}, u32[]{:S(2)}) collective-permute-start(f32[640,128]{1,0:T(8,128)S(1)} %bitcast.34), channel_id=1, source_target_pairs={{0,8},{8,0},{1,9},{9,1},{2,10},{10,2},{3,11},{11,3},{4,12},{12,4},... | collective-permute-start | bytes 983048 | tf_op jit(solution)/shard_map/ppermute | solution.py:120
